TPU v7x, 32 devices: a whole 2x2x4 slice. The times are simulated.
32 devices in a mesh: dp: 16 (over z, y, x), tensor: 2 (over core).
Axes of the slice: x: 2, y: 2, z: 4, core: 2. Of those that a mesh axis runs over, the one named last changes fastest.
Arguments:
- tokens: bfloat16 [24576, 1024], P(('dp', 'tensor')), may hold values from -6 to 6
- cotangent: bfloat16 [24576, 1024], P(('dp', 'tensor')), may hold values from -6 to 6
- lengths: int32 [16, 4], P('dp'), may hold values from 1 to 1024, 1536 in all within a row
- dealing: int32 [16, 4], P('dp'), may hold values from 0 to 3, each once within a row
- project_weight: float32 [3, 1024, 1024], P(None, 'dp', 'tensor'), may hold values from -0.1875 to 0.1875
- project_first: float32 [3, 1024, 1024], P(None, 'dp', 'tensor'), may hold values from -80 to 80
- project_second: float32 [3, 1024, 1024], P(None, 'dp', 'tensor'), may hold values from 12.288 to 49.152
- merge_weight: float32 [1024, 1024], P('tensor', 'dp'), may hold values from -3.5 to 3.5
- merge_first: float32 [1024, 1024], P('tensor', 'dp'), may hold values from -4 to 4
- merge_second: float32 [1024, 1024], P('tensor', 'dp'), may hold values from 0.072 to 0.288
- expand_weight: float32 [1024, 4096], P('dp', 'tensor'), may hold values from -0.1875 to 0.1875
- expand_first: float32 [1024, 4096], P('dp', 'tensor'), may hold values from -56 to 56
- expand_second: float32 [1024, 4096], P('dp', 'tensor'), may hold values from 6.144 to 24.576
- reduce_weight: float32 [4096, 1024], P('tensor', 'dp'), may hold values from -0.09375 to 0.09375
- reduce_first: float32 [4096, 1024], P('tensor', 'dp'), may hold values from -56 to 56
- reduce_second: float32 [4096, 1024], P('tensor', 'dp'), may hold values from 6.144 to 24.576
- vectors: float32 [8, 1024], replicated, may hold values from -1.5 to 3.33, as said below
- vector_first: float32 [8, 1024], replicated, may hold values from -112 to 112
- vector_second: float32 [8, 1024], replicated, may hold values from 24.576 to 98.304
- hidden_bias: float32 [4096], replicated, may hold values from -1.5 to 1.5
- hidden_first: float32 [4096], replicated, may hold values from -56 to 56
- hidden_second: float32 [4096], replicated, may hold values from 6.144 to 24.576
Outputs:
- encoded: bfloat16 [24576, 1024], P(('dp', 'tensor'))
- input_grad: bfloat16 [24576, 1024], P(('dp', 'tensor'))
- project_moment: float32 [3, 1024, 1024], P(None, 'dp', 'tensor')
- project_square: float32 [3, 1024, 1024], P(None, 'dp', 'tensor')
- project_master: float32 [3, 1024, 1024], P(None, 'dp', 'tensor')
- merge_moment: float32 [1024, 1024], P('tensor', 'dp')
- merge_square: float32 [1024, 1024], P('tensor', 'dp')
- merge_master: float32 [1024, 1024], P('tensor', 'dp')
- expand_moment: float32 [1024, 4096], P('dp', 'tensor')
- expand_square: float32 [1024, 4096], P('dp', 'tensor')
- expand_master: float32 [1024, 4096], P('dp', 'tensor')
- reduce_moment: float32 [4096, 1024], P('tensor', 'dp')
- reduce_square: float32 [4096, 1024], P('tensor', 'dp')
- reduce_master: float32 [4096, 1024], P('tensor', 'dp')
- vector_moment: float32 [8, 1024], replicated
- vector_square: float32 [8, 1024], replicated
- vector_master: float32 [8, 1024], replicated
- hidden_moment: float32 [4096], replicated
- hidden_square: float32 [4096], replicated
- hidden_master: float32 [4096], replicated
- vector_gradient: float32 [8, 1024], replicated
Inputs may be any that keep to these rules, and one draw needn't show every extreme that they name: Each row holds the lengths of a group's 4 sequences, summing to 1536; the longest of every row is exactly 1024. `dealing`: each row is a permutation of the numbers of a group's sequences. `vectors`: rows in order: query bias, value bias, attention output bias, first norm's gain and shift, feed-forward output bias, second norm's gain and shift; gains are positive.
All inputs are finite; a program needn't handle non-finite values.
Results may differ from a plain program's by a relative error of at most 0.02.
Values may be sent and summed in bfloat16 or wider, within the bound.
A program may use at most 256 MiB of HBM per device.

v0:
```python
import functools

import jax
import jax.numpy as jnp
from jax import lax
from jax.experimental import pallas as pl
from jax.experimental.pallas import tpu as pltpu
from jax.sharding import PartitionSpec as P

HEAD_DIM = 64
LONGEST = 1024
STEP = 10
PAIR = 2 * HEAD_DIM
TILE = 256
MIB = 1024 * 1024
MESH = pl.DeviceIdType.MESH
LOW = jnp.bfloat16
WIDE = jnp.float32

beta_one = 0.9
beta_two = 0.999
adam_epsilon = 1e-08
weight_decay = 0.01
norm_epsilon = 1e-05
masked_score = -1e30
rate_project = 0.03
rate_merge = 0.3
rate_expand = 0.03
rate_reduce = 0.015
rate_vectors = 0.4
rate_hidden = 0.1


def dot_nn(a, b):
    return jnp.dot(a, b, preferred_element_type=WIDE)


def dot_nt(a, b):
    return lax.dot_general(a, b, (((1,), (1,)), ((), ())), preferred_element_type=WIDE)


def dot_tn(a, b):
    return lax.dot_general(a, b, (((0,), (0,)), ((), ())), preferred_element_type=WIDE)


def layout(lengths_row, dealing_row, total_rows):
    slots = jnp.arange(lengths_row.shape[0], dtype=jnp.int32)
    places = jnp.arange(total_rows, dtype=jnp.int32)
    rank_of = jnp.sum(jnp.where(dealing_row[None, :] == slots[:, None], slots[None, :], 0), axis=1)
    own_start = jnp.cumsum(lengths_row) - lengths_row
    dealt_start = jnp.sum(
        jnp.where(rank_of[None, :] < rank_of[:, None], lengths_row[None, :], 0), axis=1
    )
    longest = lengths_row == LONGEST
    short = jnp.where(longest, 0, lengths_row)
    start = jnp.where(longest, 0, LONGEST + jnp.cumsum(short) - short)

    def inside(begin):
        return (places[:, None] >= begin[None, :]) & (
            places[:, None] < (begin + lengths_row)[None, :]
        )

    def moved(begin, end):
        return places + jnp.sum(jnp.where(inside(begin), (end - begin)[None, :], 0), axis=1)

    segment = jnp.sum(jnp.where(inside(start), slots[None, :], 0), axis=1)
    return (
        segment,
        moved(start, own_start),
        moved(start, dealt_start),
        moved(own_start, start),
        moved(dealt_start, start),
    )


def pick_rows(index, rows):
    places = jnp.arange(rows, dtype=jnp.int32)
    return (index[:, None] == places[None, :]).astype(LOW)


class Group:
    def __init__(self, lengths_ref, dealing_ref):
        count = lengths_ref.shape[1]
        self.lengths = [lengths_ref[0, s] for s in range(count)]
        order = [dealing_ref[0, i] for i in range(count)]
        rank = [sum(jnp.where(order[i] == s, i, 0) for i in range(count)) for s in range(count)]
        short = [jnp.where(length == LONGEST, 0, length) for length in self.lengths]
        self.own, self.dealt, self.first = [], [], []
        own = own_short = jnp.int32(0)
        for s in range(count):
            self.own.append(own)
            self.first.append(jnp.where(self.lengths[s] == LONGEST, 0, LONGEST + own_short))
            self.dealt.append(
                sum(jnp.where(rank[j] < rank[s], self.lengths[j], 0) for j in range(count))
            )
            own, own_short = own + self.lengths[s], own_short + short[s]

    def inside(self, places, begin, s):
        return (places >= begin[s]) & (places < begin[s] + self.lengths[s])

    def moved(self, places, begin, end):
        total = places
        for s in range(len(begin)):
            total = total + jnp.where(self.inside(places, begin, s), end[s] - begin[s], 0)
        return total

    def score_bias(self, count):
        sides = []
        for shape, axis in (((count, 1), 0), ((1, count), 1)):
            places = lax.broadcasted_iota(jnp.int32, shape, axis) + LONGEST
            segment = jnp.zeros_like(places)
            for s in range(len(self.first)):
                segment = segment + jnp.where(self.inside(places, self.first, s), s, 0)
            sides.append(segment)
        return jnp.where(sides[0] == sides[1], 0.0, masked_score).astype(WIDE)


def picked_rows(index, source):
    places = lax.broadcasted_iota(jnp.int32, (index.shape[0], source.shape[0]), 1)
    return dot_nn(jnp.where(index == places, 1.0, 0.0).astype(LOW), source[...])


def attend_tile(qkv_ref, pair, bias_ref, begin, size, step, context_ref, columns, total_ref):
    lane = lax.broadcasted_iota(jnp.int32, (1, PAIR), 1)
    scale = HEAD_DIM ** (-0.5)
    first = pl.multiple_of(begin + step * TILE, TILE)
    query = qkv_ref[pair, pl.ds(first, TILE), 0:PAIR]
    key = qkv_ref[pair, begin : begin + size, PAIR : 2 * PAIR]
    value = qkv_ref[pair, begin : begin + size, 2 * PAIR : 3 * PAIR]
    outcome = []
    chosen = [jnp.where(lane // HEAD_DIM == head, scale, 0.0).astype(LOW) for head in range(2)]
    scores = [dot_nt(query * chosen[head], key) for head in range(2)]
    for head in range(2):
        score = scores[head]
        if begin:
            inner = pl.multiple_of(step * TILE, TILE)
            score = score + bias_ref[pl.ds(inner, TILE), :]
        top = jnp.max(score, axis=1, keepdims=True)
        exponent = jnp.exp(score - top)
        total = jnp.sum(exponent, axis=1, keepdims=True)
        outcome.append(dot_nn(exponent.astype(LOW), value) / total)
        log_total = jnp.broadcast_to(top + jnp.log(total), (TILE, PAIR))
        total_ref[pair, head : head + 1, pl.ds(first, TILE)] = log_total.T[0:1, :]
    context_ref[pl.ds(first, TILE), columns] = jnp.where(
        lane < HEAD_DIM, outcome[0], outcome[1]
    ).astype(LOW)


def attend_kernel(qkv_ref, bias_ref, context_ref, total_ref):
    rows = qkv_ref.shape[1]
    for begin, size in ((0, LONGEST), (LONGEST, rows - LONGEST)):

        @pl.loop(0, size // TILE)
        def _(step):
            attend_tile(
                qkv_ref, 0, bias_ref, begin, size, step, context_ref, slice(0, PAIR), total_ref
            )


def attend(qkv, bias):
    pairs, rows, width = qkv.shape
    return pl.pallas_call(
        attend_kernel,
        grid=(pairs,),
        in_specs=[
            pl.BlockSpec((1, rows, width), lambda p: (p, 0, 0)),
            pl.BlockSpec(bias.shape, lambda p: (0, 0)),
        ],
        out_specs=[
            pl.BlockSpec((rows, PAIR), lambda p: (0, p)),
            pl.BlockSpec((1, 8, rows), lambda p: (p, 0, 0)),
        ],
        out_shape=[
            jax.ShapeDtypeStruct((rows, pairs * PAIR), LOW),
            jax.ShapeDtypeStruct((pairs, 8, rows), WIDE),
        ],
        compiler_params=pltpu.CompilerParams(vmem_limit_bytes=48 * MIB),
    )(qkv, bias)


def attend_back_open(qkv_ref, context_ref, upper_ref, dots, key_turned, queries, uppers):
    lane = lax.broadcasted_iota(jnp.int32, (1, PAIR), 1)
    product = (upper_ref[...].astype(WIDE) * context_ref[...].astype(WIDE)).T
    for head in range(2):
        band = slice(head * HEAD_DIM, (head + 1) * HEAD_DIM)
        dots[head : head + 1, :] = jnp.sum(product[band, :], axis=0, keepdims=True)
        chosen = lane // HEAD_DIM == head
        queries[head] = qkv_ref[:, 0:PAIR] * jnp.where(chosen, HEAD_DIM ** (-0.5), 0.0).astype(LOW)
        uppers[head] = upper_ref[...] * jnp.where(chosen, 1.0, 0.0).astype(LOW)
    key_turned[...] = qkv_ref[:, PAIR : 2 * PAIR].astype(WIDE).T.astype(LOW)


def attend_back_tile(
    qkv_ref, bias_ref, total_ref, dots, key_turned, queries, uppers, query_sum, begin, size, step
):
    block = slice(begin, begin + size)
    first = pl.multiple_of(begin + step * TILE, TILE)
    key = qkv_ref[pl.ds(first, TILE), PAIR : 2 * PAIR]
    value = qkv_ref[pl.ds(first, TILE), 2 * PAIR : 3 * PAIR]
    key_sum = jnp.zeros((TILE, PAIR), WIDE)
    value_sum = jnp.zeros((TILE, PAIR), WIDE)
    scores = [dot_nt(key, queries[head, block, :]) for head in range(2)]
    weight_grads = [dot_nt(value, uppers[head, block, :]) for head in range(2)]
    for head in range(2):
        band = slice(head * HEAD_DIM, (head + 1) * HEAD_DIM)
        score = scores[head]
        if begin:
            inner = pl.multiple_of(step * TILE, TILE)
            score = score + bias_ref[pl.ds(inner, TILE), :]
        probability = jnp.exp(score - total_ref[head : head + 1, block])
        score_grads = probability * (weight_grads[head] - dots[head : head + 1, block])
        score_grads = score_grads.astype(LOW)
        value_sum = value_sum + dot_nn(probability.astype(LOW), uppers[head, block, :])
        key_sum = key_sum + dot_nn(score_grads, queries[head, block, :])
        query_sum[band, block] += dot_nn(key_turned[band, pl.ds(first, TILE)], score_grads)
    return pl.ds(first, TILE), key_sum, value_sum


def attend_back_kernel(
    qkv_ref, bias_ref, context_ref, grad_ref, total_ref, out_ref, dots, key_turned, queries, uppers, query_sum
):
    rows = qkv_ref.shape[1]
    qkv = qkv_ref.at[0]
    attend_back_open(qkv, context_ref, grad_ref, dots, key_turned, queries, uppers)
    for begin, size in ((0, LONGEST), (LONGEST, rows - LONGEST)):
        block = slice(begin, begin + size)
        query_sum[:, block] = jnp.zeros((PAIR, size), WIDE)

        @pl.loop(0, size // TILE)
        def _(step):
            at, key_sum, value_sum = attend_back_tile(
                qkv, bias_ref, total_ref.at[0], dots, key_turned, queries, uppers, query_sum, begin, size, step
            )
            out_ref[0, at, PAIR : 2 * PAIR] = key_sum.astype(LOW)
            out_ref[0, at, 2 * PAIR : 3 * PAIR] = value_sum.astype(LOW)

        out_ref[0, block, 0:PAIR] = (query_sum[:, block] * HEAD_DIM ** (-0.5)).T.astype(LOW)


def attend_back(qkv, bias, context, grad, totals):
    pairs, rows, width = qkv.shape
    return pl.pallas_call(
        attend_back_kernel,
        grid=(pairs,),
        in_specs=[
            pl.BlockSpec((1, rows, width), lambda p: (p, 0, 0)),
            pl.BlockSpec(bias.shape, lambda p: (0, 0)),
            pl.BlockSpec((rows, PAIR), lambda p: (0, p)),
            pl.BlockSpec((rows, PAIR), lambda p: (0, p)),
            pl.BlockSpec((1, 8, rows), lambda p: (p, 0, 0)),
        ],
        out_specs=pl.BlockSpec((1, rows, width), lambda p: (p, 0, 0)),
        out_shape=jax.ShapeDtypeStruct(qkv.shape, LOW),
        scratch_shapes=[
            pltpu.VMEM((8, rows), WIDE),
            pltpu.VMEM((PAIR, rows), LOW),
            pltpu.VMEM((2, rows, PAIR), LOW),
            pltpu.VMEM((2, rows, PAIR), LOW),
            pltpu.VMEM((PAIR, rows), WIDE),
        ],
        compiler_params=pltpu.CompilerParams(vmem_limit_bytes=48 * MIB),
    )(qkv, bias, context, grad, totals)


def place():
    me = lax.axis_index("dp")
    z, y, x = me // 4, (me // 2) % 2, me % 2
    return me, z, y, x


def line_slots(z, depth):
    slots = []
    for step in range(depth - 1):
        slots.append((z - 1 - step, z - 1 - step >= 0, 1))
        slots.append((z + 1 + step, z + 1 + step < depth, -1))
    return slots


def remote(source, target, send, receive, device):
    return pltpu.make_async_remote_copy(
        src_ref=source,
        dst_ref=target,
        send_sem=send,
        recv_sem=receive,
        device_id={"dp": device},
        device_id_type=MESH,
    )


def greet_line(me, z, y, x, depth, extra=()):
    barrier = pltpu.get_barrier_semaphore()
    for peer in (z * 4 + y * 2 + 1 - x, z * 4 + (1 - y) * 2 + x):
        pl.semaphore_signal(barrier, inc=1, device_id={"dp": peer}, device_id_type=MESH)

    @pl.when(z > 0)
    def _():
        pl.semaphore_signal(barrier, inc=1, device_id={"dp": me - 4}, device_id_type=MESH)

    @pl.when(z < depth - 1)
    def _():
        pl.semaphore_signal(barrier, inc=1, device_id={"dp": me + 4}, device_id_type=MESH)

    for peer in extra:
        pl.semaphore_signal(barrier, inc=1, device_id=peer, device_id_type=MESH)
    ends = jnp.where(z > 0, 1, 0) + jnp.where(z < depth - 1, 1, 0)
    pl.semaphore_wait(barrier, 2 + len(extra) + ends)


def other_core(source, target, send, receive):
    return pltpu.make_async_remote_copy(
        src_ref=source,
        dst_ref=target,
        send_sem=send,
        recv_sem=receive,
        device_id={"tensor": 1 - lax.axis_index("tensor")},
        device_id_type=MESH,
    )


class Gather:
    def __init__(self, depth, parts, whole, far, table, sems):
        self.whole, self.far = whole, far
        self.depth = depth
        self.me, self.z, self.y, self.x = place()
        self.x_peer = self.z * 4 + self.y * 2 + 1 - self.x
        self.y_peer = self.z * 4 + (1 - self.y) * 2 + self.x
        self.rows = whole.shape[1] // parts
        self.array = [array for array, *_ in table]
        self.a, self.b, self.ab, self.c, self.all = [], [], [], [], []
        for _, base, width, third in table:
            side = (width - third) // 2
            self.a.append((base, side))
            self.b.append((base + side, side))
            self.ab.append((base, 2 * side))
            self.c.append((base + 2 * side, third))
            self.all.append((base, width))
        (
            self.z_send, self.z_recv, self.zc_send, self.zc_recv, self.xa_send, self.xa_recv, self.yb_send, self.yb_recv,
            self.ya_send, self.ya_recv, self.xb_send, self.xb_recv, self.c_send, self.c_recv, self.far_send, self.far_recv,
        ) = sems
        self.slots = line_slots(self.z, depth)

    @staticmethod
    def semaphores(depth, pieces):
        sem = pltpu.SemaphoreType.DMA
        return [
            *[sem((pieces, depth + 1)), sem((pieces, depth))] * 2,
            *[sem((pieces,)), sem((pieces, depth))] * 2,
            *[sem((pieces,)), sem((pieces, depth, 2))] * 2,
            sem((pieces, 2)),
            sem((pieces, 2)),
            sem((pieces,)),
            sem((pieces,)),
        ]

    def block(self, zb, yb, xb):
        return zb * 4 + yb * 2 + xb

    def cut(self, ref, p, block, count, columns):
        first = pl.multiple_of(block * self.rows, self.rows)
        return ref.at[self.array[p], pl.ds(first, count * self.rows), pl.ds(*columns)]

    def copy(self, p, block, count, columns, send, receive, device):
        part = self.cut(self.whole, p, block, count, columns)
        return remote(part, part, send, receive, device)

    def forward(self, p, block, count, columns):
        if p == 0:
            return
        other_core(
            self.cut(self.whole, p, block, count, columns),
            self.cut(self.far, p, block, count, columns),
            self.far_send.at[p],
            self.far_recv.at[p],
        ).start()

    def far_copy(self, p):
        part = self.far.at[self.array[p], :, pl.ds(*self.all[p])]
        return other_core(part, part, self.far_send.at[p], self.far_recv.at[p])

    def z_copy(self, p, zb, way, back=False):
        block = self.block(zb, self.y, self.x)
        sem = self.depth if back else zb
        return self.copy(
            p, block, 1, self.ab[p], self.z_send.at[p, sem], self.z_recv.at[p, zb], self.me + 4 * way
        )

    def zc_copy(self, p, zb, way, back=False):
        sem = self.depth if back else zb
        return self.copy(
            p, zb * 4, 4, self.c[p], self.zc_send.at[p, sem], self.zc_recv.at[p, zb], self.me + 4 * way
        )

    def xa(self, p, zb, xb):
        block = self.block(zb, self.y, xb)
        return self.copy(
            p, block, 1, self.a[p], self.xa_send.at[p], self.xa_recv.at[p, zb], self.x_peer
        )

    def yb(self, p, zb, yb):
        block = self.block(zb, yb, self.x)
        return self.copy(
            p, block, 1, self.b[p], self.yb_send.at[p], self.yb_recv.at[p, zb], self.y_peer
        )

    def ya(self, p, zb, yb, xb):
        block = self.block(zb, yb, xb)
        return self.copy(
            p, block, 1, self.a[p], self.ya_send.at[p], self.ya_recv.at[p, zb, xb], self.y_peer
        )

    def xb(self, p, zb, yb, xb):
        block = self.block(zb, yb, xb)
        return self.copy(
            p, block, 1, self.b[p], self.xb_send.at[p], self.xb_recv.at[p, zb, yb], self.x_peer
        )

    def xc(self, p, xb):
        block = self.block(self.z, self.y, xb)
        return self.copy(
            p, block, 1, self.c[p], self.c_send.at[p, 0], self.c_recv.at[p, 0], self.x_peer
        )

    def yc(self, p, yb):
        block = self.block(self.z, yb, 0)
        return self.copy(
            p, block, 2, self.c[p], self.c_send.at[p, 1], self.c_recv.at[p, 1], self.y_peer
        )

    def both_ways(self, copy, act):
        @pl.when(self.z < self.depth - 1)
        def _():
            act(copy(self.z, 1))

        @pl.when(self.z > 0)
        def _():
            act(copy(self.z, -1, True))

    def spread(self, p, zb):
        self.xa(p, zb, self.x).start()
        self.yb(p, zb, self.y).start()
        self.ya(p, zb, self.y, self.x).start()
        self.xb(p, zb, self.y, self.x).start()

    def turn(self, p, zb):
        self.xa(p, zb, 1 - self.x).wait_recv()
        self.ya(p, zb, self.y, 1 - self.x).start()
        self.forward(p, self.block(zb, self.y, 1 - self.x), 1, self.a[p])
        self.yb(p, zb, 1 - self.y).wait_recv()
        self.xb(p, zb, 1 - self.y, self.x).start()
        self.forward(p, self.block(zb, 1 - self.y, self.x), 1, self.b[p])

    def at_step(self, step, act):
        for zb, valid, way in self.slots[2 * step : 2 * step + 2]:
            on = (self.z + way >= 0) & (self.z + way < self.depth)
            pl.when(valid)(functools.partial(act, zb, way, on))

    def arrive(self, p, step):
        def act(zb, way, on):
            self.z_copy(p, zb, way).wait_recv()
            pl.when(on)(lambda: self.z_copy(p, zb, way).start())
            self.spread(p, zb)
            self.forward(p, self.block(zb, self.y, self.x), 1, self.ab[p])

        self.at_step(step, act)

    def arrive_c(self, p, step):
        def act(zb, way, on):
            self.zc_copy(p, zb, way).wait_recv()
            pl.when(on)(lambda: self.zc_copy(p, zb, way).start())
            self.forward(p, zb * 4, 4, self.c[p])

        self.at_step(step, act)

    def stage(self, p, s):
        depth = self.depth
        if s == 0:
            self.both_ways(lambda *way: self.z_copy(p, *way), lambda copy: copy.start())
            self.xc(p, self.x).start()
            self.spread(p, self.z)
            self.forward(p, self.me, 1, self.all[p])
            return
        if s == 1:
            self.xc(p, 1 - self.x).wait_recv()
            self.yc(p, self.y).start()
            self.forward(p, self.block(self.z, self.y, 1 - self.x), 1, self.c[p])
        if s == 2:
            self.yc(p, 1 - self.y).wait_recv()
            self.both_ways(lambda *way: self.zc_copy(p, *way), lambda copy: copy.start())
            self.forward(p, self.block(self.z, 1 - self.y, 0), 2, self.c[p])
        if 1 <= s < depth:
            self.arrive(p, s - 1)
        if 3 <= s < depth + 2:
            self.arrive_c(p, s - 3)
        if s == 2:
            self.turn(p, self.z)
        if 3 <= s < depth + 2:
            self.at_step(s - 3, lambda zb, way, on: self.turn(p, zb))
        if s == depth + 2:
            for zb in range(depth):
                for other in range(2):
                    self.ya(p, zb, 1 - self.y, other).wait_recv()
                self.forward(p, self.block(zb, 1 - self.y, 0), 2, self.a[p])
                for other in range(2):
                    self.xb(p, zb, other, 1 - self.x).wait_recv()
                    self.forward(p, self.block(zb, other, 1 - self.x), 1, self.b[p])

    def finish(self, p):
        def sent(copy):
            copy.wait_send()

        if p:
            self.far_copy(p).wait_send()
        self.both_ways(lambda *way: self.z_copy(p, *way), sent)
        self.both_ways(lambda *way: self.zc_copy(p, *way), sent)
        for count, columns, sem in (
            (1, self.a[p], self.xa_send),
            (1, self.b[p], self.yb_send),
            (2, self.a[p], self.ya_send),
            (2, self.b[p], self.xb_send),
        ):
            part = self.cut(self.whole, p, 0, count * self.depth, columns)
            remote(part, part, sem.at[p], sem.at[p], self.me).wait_send()
        self.xc(p, self.x).wait_send()
        self.yc(p, self.y).wait_send()

        def passed(zb, way, on):
            pl.when(on)(lambda: sent(self.z_copy(p, zb, way)))
            pl.when(on)(lambda: sent(self.zc_copy(p, zb, way)))

        for step in range(self.depth - 1):
            self.at_step(step, passed)


def looped(count, body, between):
    @pl.loop(0, count)
    def _(i):
        body(i)
        for step, acts in between.items():

            @pl.when(i == step)
            def _():
                for act in acts:
                    act()


GATHER_AT = {
    "hidden": {0: [(2, 0), (1, 0)], 1: [(0, 1), (0, 2), (0, 3)], 3: [(0, 4)], 4: [(0, 5), (1, 1)]},
    "upstream": {-1: [(2, 1)], 1: [(3, 0)]},
    "project": {-1: [(4, 0), (0, 6)], 1: [(1, 2)], 5: [(2, 2)]},
    "long": {2: [(3, 1), (1, 3)], 7: [(2, 3)], 9: [(1, 4)], 14: [(2, 4)]},
    "short": {2: [(1, 5)], 3: [(3, 2)], 5: [(4, 1)]},
    "norm": {-1: [(1, 6)], 1: [(2, 5)], 3: [(3, 3)]},
    "feed": {-1: [(4, 2), (2, 6)], 0: [(3, 4)], 1: [(4, 3)], 2: [(3, 5)]},
    "last": {-1: [(3, 6), (4, 4)], 0: [(4, 5)]},
    "tail": {-1: [(4, 6)]},
}


def piece_table(width, inner):
    third = width // 8
    return (
        (0, 0, 3 * inner, third),
        (0, 3 * inner, inner, third),
        (1, 0, width, 2 * third),
        (2, 0, width // 2, third),
        (2, width // 2, width // 2, third),
    )


def chunk_columns(j, per_piece, half):
    array, at = 1 + j // per_piece, j % per_piece
    pair = per_piece // 2
    quarter = (at // pair) * per_piece * half + (at % pair) * half
    if isinstance(j, int):
        split = array > 1
        return array, quarter if split else at * half, (
            quarter + pair * half if split else (per_piece + at) * half
        )
    split = array > 1
    first = jnp.where(split, quarter, at * half)
    return array, first, first + jnp.where(split, pair, per_piece) * half


def front_kernel(
    depth, lengths_ref, dealing_ref, project_in, merge_in, expand_in, reduce_in, vectors_in, hidden_bias_in,
    tokens_ref, cotangent_ref,
    whole_out, far_ref, qkv_out, turned_out, upstream_out, context_out, total_out,
    acc_out, normal_out, inverse_out, low_turned_out, active_out, slope_out, far_context_out,
    project_ref, merge_ref, expand_ref, reduce_ref, vectors_ref, hidden_bias_ref,
    whole, score_bias, token, upper, hidden, turned, upstream, qkv, context, total,
    acc, normal, inverse, low, low_turned, active, slope, far_context, merge_far, expand_buf, reduce_buf,
    local_sem, core_sem, out_sem, load_sem, chunk_sem, weight_sem, *sems,
):
    arrays = whole.shape[0]
    half_rows, width = tokens_ref.shape
    rows = 2 * half_rows
    pairs = qkv.shape[0]
    inner = pairs * PAIR
    both = expand_buf.shape[2]
    half = both // 2
    hidden_half = expand_ref.shape[1]
    chunks = hidden_half // half
    per_piece = chunks // (arrays - 1)
    member = lax.axis_index("tensor")
    table = piece_table(whole.shape[2], inner)
    pieces = len(table)
    lines = Gather(depth, 4 * depth, whole, far_ref, table, sems)
    me = lines.me
    tall, short = 2 * TILE, TILE // 2

    weights = [
        pltpu.make_async_copy(source, target, weight_sem.at[i])
        for i, (source, target) in enumerate(
            (
                (project_in, project_ref),
                (merge_in, merge_ref),
                (expand_in, expand_ref),
                (reduce_in, reduce_ref),
                (vectors_in, vectors_ref),
                (hidden_bias_in, hidden_bias_ref),
            )
        )
    ]
    for copy in weights:
        copy.start()
    own = [
        pltpu.make_async_copy(tokens_ref, token.at[member], local_sem.at[0]),
        pltpu.make_async_copy(cotangent_ref, upper.at[member], local_sem.at[1]),
    ]
    for copy in own:
        copy.start()
    for copy in weights:
        copy.wait()
    mine = pl.ds(pl.multiple_of(me * lines.rows, lines.rows), lines.rows)
    for pair in range(pairs):
        for c in range(3):
            first = (3 * pair + c) * PAIR
            whole[0, mine, first : first + PAIR] = project_ref[
                c, :, pair * PAIR : (pair + 1) * PAIR
            ].astype(LOW)
    whole[0, mine, 3 * inner :] = merge_ref[...].astype(LOW)
    for j in range(chunks):
        array, first, second = chunk_columns(j, per_piece, half)
        columns = slice(j * half, (j + 1) * half)
        whole[array, mine, first : first + half] = expand_ref[:, columns].astype(LOW)
        whole[array, mine, second : second + half] = reduce_ref[:, columns].astype(LOW)
    greet_line(me, lines.z, lines.y, lines.x, depth, [{"tensor": 1 - member}])
    crossing = [
        other_core(tokens_ref, token.at[member], core_sem.at[0, 0], core_sem.at[0, 1]),
        other_core(cotangent_ref, upper.at[member], core_sem.at[1, 0], core_sem.at[1, 1]),
    ]
    lines.stage(0, 0)
    for copy in crossing:
        copy.start()
    group = Group(lengths_ref, dealing_ref)
    score_bias[...] = group.score_bias(rows - LONGEST)
    for copy in own:
        copy.wait()

    leaving = []

    def leave(source, target):
        copy = pltpu.make_async_copy(source, target, out_sem.at[len(leaving)])
        copy.start()
        leaving.append(copy)

    def before(name):
        for stage in GATHER_AT.get(name, {}).get(-1, ()):
            lines.stage(*stage)

    def phase(name, count, body):
        between = {
            step: [functools.partial(lines.stage, *stage) for stage in stages]
            for step, stages in GATHER_AT.get(name, {}).items()
            if step >= 0
        }
        looped(count, body, between)

    def places_of(first):
        return first + lax.broadcasted_iota(jnp.int32, (TILE, 1), 0)

    def picked(index, source):
        return picked_rows(index, source.at[0]) + picked_rows(index - half_rows, source.at[1])

    def tile(step, size=TILE):
        return pl.ds(pl.multiple_of(step * size, size), size)

    def hidden_tile(step):
        index = group.moved(places_of(step * TILE), group.first, group.own)
        rows_here = picked(index, token)
        hidden[tile(step), :] = rows_here.astype(LOW)
        turned[:, tile(step)] = rows_here.T.astype(LOW)

    def upstream_tile(step):
        places = places_of(member * half_rows + step * TILE)
        index = group.moved(places, group.first, group.dealt)
        upstream[tile(step), :] = picked(index, upper).astype(LOW)

    crossing[0].wait()
    before("hidden")
    phase("hidden", rows // TILE, hidden_tile)
    leave(turned, turned_out)
    crossing[1].wait()
    before("upstream")
    phase("upstream", half_rows // TILE, upstream_tile)
    leave(upstream, upstream_out)

    def project_tile(i):
        pair, step = i // (rows // tall), lax.rem(i, rows // tall)
        at = tile(step, tall)
        columns = pl.ds(pl.multiple_of(pair * 3 * PAIR, PAIR), 3 * PAIR)
        bias_columns = pl.ds(pl.multiple_of(member * inner + pair * PAIR, PAIR), PAIR)
        bias = jnp.concatenate(
            [
                vectors_ref[0:1, bias_columns],
                jnp.zeros((1, PAIR), WIDE),
                vectors_ref[1:2, bias_columns],
            ],
            axis=1,
        )
        qkv[pair, at, :] = (dot_nn(hidden[at, :], whole[0, :, columns]) + bias).astype(LOW)

    before("project")
    phase("project", pairs * rows // tall, project_tile)
    leave(qkv, qkv_out)

    def attend_step(begin, size):
        def step_of(i):
            pair, step = i // (size // TILE), lax.rem(i, size // TILE)
            columns = pl.ds(pl.multiple_of(pair * PAIR, PAIR), PAIR)
            attend_tile(qkv, pair, score_bias, begin, size, step, context, columns, total)

        return step_of

    before("long")
    phase("long", pairs * LONGEST // TILE, attend_step(0, LONGEST))
    before("short")
    phase("short", pairs * (rows - LONGEST) // TILE, attend_step(LONGEST, rows - LONGEST))
    leave(context, context_out)
    leave(total, total_out)

    own_first = member * half_rows
    other_rows = pl.ds(pl.multiple_of((1 - member) * half_rows, half_rows), half_rows)
    crossing = other_core(context.at[other_rows], far_context, core_sem.at[2, 0], core_sem.at[2, 1])
    crossing.start()
    before("norm")
    lines.far_copy(1).wait_recv()
    merge_columns = pl.ds(whole.shape[2] - inner, inner)
    merge_copy = pltpu.make_async_copy(
        far_ref.at[0, :, merge_columns], merge_far, local_sem.at[2]
    )
    merge_copy.start()
    merge_copy.wait()
    crossing.wait()
    leave(far_context, far_context_out)

    def norm_tile(step):
        at = tile(step, short)
        own_at = pl.ds(pl.multiple_of(own_first + step * short, short), short)
        branch = dot_nt(context[own_at, :], whole[0, :, merge_columns])
        branch = branch + dot_nt(far_context[at, :], merge_far[...])
        unit, scale = norm(hidden[own_at, :].astype(WIDE) + branch + vectors_ref[2:3, :])
        normed = unit * vectors_ref[3:4, :] + vectors_ref[4:5, :]
        normal[at, :] = unit
        inverse[at, :] = jnp.broadcast_to(scale, (short, 128))
        low[at, :] = normed.astype(LOW)
        low_turned[:, at] = normed.T.astype(LOW)
        acc[at, :] = normed + vectors_ref[5:6, :]

    leave(whole.at[0], whole_out.at[0])
    phase("norm", half_rows // short, norm_tile)
    leave(normal, normal_out)
    leave(inverse, inverse_out)
    leave(low_turned, low_turned_out)

    def loads(j):
        slot = lax.rem(j, 2)
        array, *firsts = chunk_columns(j, per_piece, half)
        copies = []
        for kind, buf in enumerate((expand_buf, reduce_buf)):
            first = pl.multiple_of(firsts[kind], half)
            for side, source in enumerate((far_ref, whole)):
                copies.append(
                    pltpu.make_async_copy(
                        source.at[array, :, pl.ds(first, half)],
                        buf.at[slot, :, pl.ds(side * half, half)],
                        load_sem.at[slot, kind, side],
                    )
                )
        return copies

    def results(j):
        slot = lax.rem(j, 2)
        return [
            pltpu.make_async_copy(active.at[slot], active_out.at[j], chunk_sem.at[slot, 0]),
            pltpu.make_async_copy(slope.at[slot], slope_out.at[j], chunk_sem.at[slot, 1]),
        ]

    def chunk_of(piece, first_chunk, count):
        def chunk(i):
            j = first_chunk + i
            slot = lax.rem(j, 2)

            @pl.when(i == 0)
            def _():
                lines.far_copy(piece).wait_recv()
                for copy in loads(j):
                    copy.start()

            for copy in loads(j):
                copy.wait()

            @pl.when(i + 1 < count)
            def _():
                for copy in loads(j + 1):
                    copy.start()

            @pl.when(j >= 2)
            def _():
                for copy in results(j - 2):
                    copy.wait()

            biases = []
            for which in (1 - member, member):
                first = pl.multiple_of(which * hidden_half + j * half, half)
                biases.append(hidden_bias_ref[:, pl.ds(first, half)])
            bias = jnp.concatenate(biases, axis=1)
            tiles = [slice(step * TILE, (step + 1) * TILE) for step in range(half_rows // TILE)]
            parts = [dot_nn(low[at, :], expand_buf[slot]) for at in tiles]
            for at, part in zip(tiles, parts, strict=True):
                value = part + bias
                below, bell = normal_cells(value)
                held = (value * below).astype(LOW)
                active[slot, at, :] = held
                slope[slot, at, :] = (below + value * bell * 0.3989422804014327).astype(LOW)
                acc[at, :] += dot_nt(held, reduce_buf[slot])
            for copy in results(j):
                copy.start()

        return chunk

    first_chunk = 0
    for piece, name in ((2, "feed"), (3, "last"), (4, "tail")):
        count = chunks * table[piece][2] // (2 * hidden_half)
        before(name)
        columns = pl.ds(*lines.all[piece])
        leave(
            whole.at[lines.array[piece], :, columns],
            whole_out.at[lines.array[piece], :, columns],
        )
        if name == "last":
            for p in range(piece):
                lines.finish(p)
        phase(name, count, chunk_of(piece, first_chunk, count))
        first_chunk += count
    leave(acc, acc_out)
    for p in range(pieces - 2, pieces):
        lines.finish(p)
    for j in (chunks - 2, chunks - 1):
        for copy in results(j):
            copy.wait()
    for copy in leaving:
        copy.wait()


def front(lengths, dealing, project, merge, expand, reduce, vectors, hidden_bias, tokens, cotangent, parts):
    shard_rows, hidden_half = expand.shape
    arrays, columns = 3, hidden_half
    half_rows, width = tokens.shape
    rows, pairs, depth = 2 * half_rows, project.shape[2] // PAIR, parts // 4
    inner, half = pairs * PAIR, 256
    pieces = len(piece_table(columns, inner))
    chunks, both = hidden_half // half, 2 * half
    shape, sem = jax.ShapeDtypeStruct, pltpu.SemaphoreType.DMA
    anywhere = pl.BlockSpec(memory_space=pl.ANY)
    held = [
        ((pairs, rows, 3 * PAIR), LOW),
        ((width, rows), LOW),
        ((half_rows, width), LOW),
        ((rows, inner), LOW),
        ((pairs, 8, rows), WIDE),
        ((half_rows, width), WIDE),
        ((half_rows, width), WIDE),
        ((half_rows, 128), WIDE),
        ((width, half_rows), LOW),
        ((chunks, half_rows, both), LOW),
        ((chunks, half_rows, both), LOW),
        ((half_rows, inner), LOW),
    ]
    return pl.pallas_call(
        functools.partial(front_kernel, depth),
        in_specs=[*[pl.BlockSpec(memory_space=pltpu.SMEM)] * 2, *[anywhere] * 8],
        out_specs=[anywhere] * 14,
        out_shape=[
            shape((arrays, parts * shard_rows, columns), LOW),
            shape((arrays, parts * shard_rows, columns), LOW),
            *[shape(*one) for one in held],
        ],
        scratch_shapes=[
            *[
                pltpu.VMEM(one.shape, WIDE)
                for one in (project, merge, expand, reduce, vectors, hidden_bias)
            ],
            pltpu.VMEM((arrays, parts * shard_rows, columns), LOW),
            pltpu.VMEM((rows - LONGEST, rows - LONGEST), WIDE),
            pltpu.VMEM((2, half_rows, width), LOW),
            pltpu.VMEM((2, half_rows, width), LOW),
            pltpu.VMEM((rows, width), LOW),
            pltpu.VMEM((width, rows), LOW),
            pltpu.VMEM((half_rows, width), LOW),
            pltpu.VMEM((pairs, rows, 3 * PAIR), LOW),
            pltpu.VMEM((rows, inner), LOW),
            pltpu.VMEM((pairs, 8, rows), WIDE),
            pltpu.VMEM((half_rows, width), WIDE),
            pltpu.VMEM((half_rows, width), WIDE),
            pltpu.VMEM((half_rows, 128), WIDE),
            pltpu.VMEM((half_rows, width), LOW),
            pltpu.VMEM((width, half_rows), LOW),
            pltpu.VMEM((2, half_rows, both), LOW),
            pltpu.VMEM((2, half_rows, both), LOW),
            pltpu.VMEM((half_rows, inner), LOW),
            pltpu.VMEM((width, inner), LOW),
            pltpu.VMEM((2, width, both), LOW),
            pltpu.VMEM((2, width, both), LOW),
            sem((3,)),
            sem((3, 2)),
            sem((16,)),
            sem((2, 2, 2)),
            sem((2, 2)),
            sem((6,)),
            *Gather.semaphores(depth, pieces),
        ],
        compiler_params=pltpu.CompilerParams(
            collective_id=0, has_side_effects=True, vmem_limit_bytes=63 * MIB
        ),
    )(lengths, dealing, project, merge, expand, reduce, vectors, hidden_bias, tokens, cotangent)


def normal_cells(value):
    bell = jnp.exp2(value * value * (-0.5 * 1.4426950408889634))
    below = 1.0 + 0.39 * 0.7071067811865476 * jnp.abs(value)
    t = pl.reciprocal(below, approx=True)
    t = t * (2.0 - below * t)
    t = t * (2.0 - below * t)
    tail = 0.5 * -0.2275377237624147
    for factor in (
        0.8866668177122106,
        -0.6354042576077721,
        0.649562611731642,
        0.0913871257655044,
        0.23532542445435511,
    ):
        tail = tail * t + 0.5 * factor
    tail = tail * t * bell
    return jnp.where(value < 0.0, tail, 1.0 - tail), bell


def norm(values):
    center = values - jnp.mean(values, axis=1, keepdims=True)
    spread = jnp.mean(center * center, axis=1, keepdims=True)
    scale = lax.rsqrt(spread + norm_epsilon)
    return center * scale, scale


def norm_back(scaled, unit, scale):
    return scale * (
        scaled
        - jnp.mean(scaled, axis=1, keepdims=True)
        - unit * jnp.mean(scaled * unit, axis=1, keepdims=True)
    )


def feed_kernel(
    context_ref, merge_ref, merge_far_ref, whole_ref, far_ref, hidden_ref, upstream_ref, vectors_ref, bias_ref,
    encoded_ref, branch_ref, grad_ref, merge_grad_ref, expand_grad_ref, reduce_grad_ref, sums_ref, hidden_sums_ref,
    own_ctx, far_ctx, acc, normal, inverse, low, turned, late, late_turned, active, slope, inner_grad,
    expand_buf, reduce_buf, arrived, leaving, kept, done, grad_own, grad_far, merge_send, merge_recv,
    ctx_sem, load_sem, send_sem, recv_sem, out_sem, last_sem,
):
    rows = hidden_ref.shape[0]
    chunks, _, both = bias_ref.shape
    half = both // 2
    per_piece = whole_ref.shape[2] // (2 * half)
    member = lax.axis_index("tensor")
    peer = {"tensor": 1 - member}
    tall, short = 256, 128
    width = hidden_ref.shape[1]

    def across(source, target, send, receive):
        return pltpu.make_async_remote_copy(
            src_ref=source,
            dst_ref=target,
            send_sem=send,
            recv_sem=receive,
            device_id=peer,
            device_id_type=MESH,
        )

    def rows_of(which):
        return pl.ds(pl.multiple_of(which * rows, rows), rows)

    def tile(step, size):
        return pl.ds(pl.multiple_of(step * size, size), size)

    def loads(j, slot):
        piece, at = 1 + j // per_piece, lax.rem(j, per_piece) * half
        copies = []
        for kind, buf in enumerate((expand_buf, reduce_buf)):
            first = pl.multiple_of(at + kind * per_piece * half, half)
            for side, source in enumerate((far_ref, whole_ref)):
                copies.append(
                    pltpu.make_async_copy(
                        source.at[piece, :, pl.ds(first, half)],
                        buf.at[slot, :, pl.ds(side * half, half)],
                        load_sem.at[slot, kind, side],
                    )
                )
        return copies

    for copy in loads(0, 0):
        copy.start()
    barrier = pltpu.get_barrier_semaphore()
    pl.semaphore_signal(barrier, inc=1, device_id=peer, device_id_type=MESH)
    pl.semaphore_wait(barrier, 1)
    out_ctx = across(context_ref.at[rows_of(1 - member)], far_ctx, ctx_sem.at[0], ctx_sem.at[1])
    out_ctx.start()
    in_ctx = pltpu.make_async_copy(context_ref.at[rows_of(member)], own_ctx, ctx_sem.at[2])
    in_ctx.start()
    sums_ref[...] = jnp.zeros_like(sums_ref)
    in_ctx.wait()
    out_ctx.wait()

    def add_sum(row, values):
        sums_ref[row : row + 1, :] += jnp.sum(values, axis=0, keepdims=True)

    @pl.loop(0, rows // short)
    def _(step):
        at = tile(step, short)
        branch = dot_nt(own_ctx[at, :], merge_ref[...]) + dot_nt(far_ctx[at, :], merge_far_ref[...])
        unit, scale = norm(hidden_ref[at, :].astype(WIDE) + branch + vectors_ref[2:3, :])
        normed = unit * vectors_ref[3:4, :] + vectors_ref[4:5, :]
        normal[at, :] = unit
        inverse[at, :] = jnp.broadcast_to(scale, (short, 128))
        low[at, :] = normed.astype(LOW)
        turned[:, at] = normed.T.astype(LOW)
        acc[at, :] = normed + vectors_ref[5:6, :]

    @pl.loop(0, chunks)
    def _(j):
        slot = lax.rem(j, 2)
        for copy in loads(j, slot):
            copy.wait()

        @pl.when(j + 1 < chunks)
        def _():
            for copy in loads(j + 1, 1 - slot):
                copy.start()

        for step in range(rows // tall):
            at = slice(step * tall, (step + 1) * tall)
            inner = dot_nn(low[at, :], expand_buf[slot]) + bias_ref[j]
            below, bell = normal_cells(inner)
            held = (inner * below).astype(LOW)
            active[j, at, :] = held
            slope[j, at, :] = (below + inner * bell * 0.3989422804014327).astype(LOW)
            acc[at, :] += dot_nt(held, reduce_buf[slot])

    for copy in loads(0, 0):
        copy.start()

    @pl.loop(0, rows // short)
    def _(step):
        at = tile(step, short)
        unit, scale = norm(acc[at, :])
        encoded_ref[at, :] = (unit * vectors_ref[6:7, :] + vectors_ref[7:8, :]).astype(LOW)
        upper = upstream_ref[at, :].astype(WIDE)
        add_sum(6, upper * unit)
        add_sum(7, upper)
        grad = norm_back(upper * vectors_ref[6:7, :], unit, scale)
        grad_low = grad.astype(LOW)
        add_sum(5, grad_low.astype(WIDE))
        acc[at, :] = grad
        late[at, :] = grad_low
        late_turned[:, at] = grad.T.astype(LOW)

    def send(j, kind):
        return across(
            leaving.at[lax.rem(j, 2), kind],
            arrived.at[lax.rem(j, 4), kind],
            send_sem.at[lax.rem(j, 2), kind],
            recv_sem.at[lax.rem(j, 4), kind],
        )

    def store(j, kind):
        target = (expand_grad_ref, reduce_grad_ref)[kind]
        cols = pl.ds(pl.multiple_of(j * half, half), half)
        return pltpu.make_async_copy(
            done.at[lax.rem(j, 2), kind], target.at[:, cols], out_sem.at[lax.rem(j, 2), kind]
        )

    def finish(j):
        for kind in range(2):
            send(j, kind).wait_recv()

            @pl.when(j >= 2)
            def _():
                store(j - 2, kind).wait()

            @pl.loop(0, width // tall)
            def _(step):
                at = tile(step, tall)
                done[lax.rem(j, 2), kind, at, :] = (
                    kept[lax.rem(j, 2), kind, at, :]
                    + arrived[lax.rem(j, 4), kind, at, :].astype(WIDE)
                ).astype(LOW)

            store(j, kind).start()

    @pl.loop(0, chunks)
    def _(j):
        slot = lax.rem(j, 2)
        for copy in loads(j, slot):
            copy.wait()

        @pl.when(j + 1 < chunks)
        def _():
            for copy in loads(j + 1, 1 - slot):
                copy.start()

        total = jnp.zeros((1, both), WIDE)
        for step in range(rows // tall):
            at = slice(step * tall, (step + 1) * tall)
            grad = dot_nn(late[at, :], reduce_buf[slot]) * slope[j, at, :].astype(WIDE)
            grad = grad.astype(LOW)
            inner_grad[at, :] = grad
            total = total + jnp.sum(grad.astype(WIDE), axis=0, keepdims=True)
            acc[at, :] += dot_nt(grad, expand_buf[slot])
        hidden_sums_ref[j] = total

        @pl.when(j >= 2)
        def _():
            for kind in range(2):
                send(j - 2, kind).wait_send()

        for kind, (left, right) in enumerate(((turned, inner_grad), (late_turned, active.at[j]))):
            for step in range(width // tall):
                at = slice(step * tall, (step + 1) * tall)
                part = dot_nn(left[at, :], right[...])
                leaving[slot, kind, at, :] = part[:, 0:half].astype(LOW)
                kept[slot, kind, at, :] = part[:, half:both]
            send(j, kind).start()

        @pl.when(j >= 1)
        def _():
            finish(j - 1)

    @pl.loop(0, rows // short)
    def _(step):
        at = tile(step, short)
        grad = acc[at, :]
        unit = normal[at, :]
        add_sum(3, grad * unit)
        add_sum(4, grad)
        branch_grad = norm_back(grad * vectors_ref[3:4, :], unit, inverse[at, 0:1])
        branch_low = branch_grad.astype(LOW)
        add_sum(2, branch_low.astype(WIDE))
        branch_ref[at, :] = branch_grad
        turned[:, at] = branch_grad.T.astype(LOW)
        grad_far[at, :] = dot_nn(branch_low, merge_far_ref[...]).astype(LOW)
        grad_own[at, :] = dot_nn(branch_low, merge_ref[...]).astype(LOW)

    out_grad = across(grad_far, grad_ref.at[rows_of(member)], ctx_sem.at[0], ctx_sem.at[1])
    out_grad.start()
    in_grad = pltpu.make_async_copy(grad_own, grad_ref.at[rows_of(member)], ctx_sem.at[2])
    in_grad.start()
    for step in range(width // tall):
        at = slice(step * tall, (step + 1) * tall)
        merge_send[at, :] = dot_nn(turned[at, :], far_ctx[...]).astype(LOW)
    out_merge = across(merge_send, merge_recv, last_sem.at[0], last_sem.at[1])
    out_merge.start()
    finish(chunks - 1)
    for kind in range(2):
        send(chunks - 2, kind).wait_send()
        send(chunks - 1, kind).wait_send()
        store(chunks - 2, kind).wait()
        store(chunks - 1, kind).wait()
    out_merge.wait()
    for step in range(width // tall):
        at = slice(step * tall, (step + 1) * tall)
        merge_grad_ref[at, :] = (
            dot_nn(turned[at, :], own_ctx[...]) + merge_recv[at, :].astype(WIDE)
        ).astype(LOW)
    out_grad.wait()
    in_grad.wait()


def feed_block(context, whole, far, hidden_own, upstream, vectors, bias_own, bias_far):
    total_rows, inner = context.shape
    rows, width = hidden_own.shape
    hidden = bias_own.shape[0]
    merge, merge_far = whole[0, :, -inner:], far[0, :, -inner:]
    half = 256
    chunks = hidden // half
    both = 2 * half
    bias = jnp.concatenate(
        [bias_far.reshape(chunks, 1, half), bias_own.reshape(chunks, 1, half)], axis=2
    )
    vmem, anywhere = pl.BlockSpec(memory_space=pltpu.VMEM), pl.BlockSpec(memory_space=pl.ANY)
    sem = pltpu.SemaphoreType.DMA
    shape = jax.ShapeDtypeStruct
    *results, hidden_sums = pl.pallas_call(
        feed_kernel,
        in_specs=[anywhere, vmem, vmem, *[anywhere] * 2, *[vmem] * 4],
        out_specs=[vmem, vmem, anywhere, vmem, anywhere, anywhere, vmem, vmem],
        out_shape=[
            shape((rows, width), LOW),
            shape((rows, width), WIDE),
            shape((total_rows, inner), LOW),
            shape((width, inner), LOW),
            shape((width, hidden), LOW),
            shape((width, hidden), LOW),
            shape((8, width), WIDE),
            shape((chunks, 1, both), WIDE),
        ],
        scratch_shapes=[
            pltpu.VMEM((rows, inner), LOW),
            pltpu.VMEM((rows, inner), LOW),
            pltpu.VMEM((rows, width), WIDE),
            pltpu.VMEM((rows, width), WIDE),
            pltpu.VMEM((rows, 128), WIDE),
            pltpu.VMEM((rows, width), LOW),
            pltpu.VMEM((width, rows), LOW),
            pltpu.VMEM((rows, width), LOW),
            pltpu.VMEM((width, rows), LOW),
            pltpu.VMEM((chunks, rows, both), LOW),
            pltpu.VMEM((chunks, rows, both), LOW),
            pltpu.VMEM((rows, both), LOW),
            pltpu.VMEM((2, width, both), LOW),
            pltpu.VMEM((2, width, both), LOW),
            pltpu.VMEM((4, 2, width, half), LOW),
            pltpu.VMEM((2, 2, width, half), LOW),
            pltpu.VMEM((2, 2, width, half), WIDE),
            pltpu.VMEM((2, 2, width, half), LOW),
            pltpu.VMEM((rows, inner), LOW),
            pltpu.VMEM((rows, inner), LOW),
            pltpu.VMEM((width, inner), LOW),
            pltpu.VMEM((width, inner), LOW),
            sem((3,)),
            sem((2, 2, 2)),
            sem((2, 2)),
            sem((4, 2)),
            sem((2, 2)),
            sem((2,)),
        ],
        compiler_params=pltpu.CompilerParams(
            collective_id=2, has_side_effects=True, vmem_limit_bytes=60 * MIB
        ),
        cost_estimate=pl.CostEstimate(
            flops=12 * rows * width * 2 * hidden, bytes_accessed=8 * width * hidden * 4, transcendentals=0
        ),
    )(context, merge, merge_far, whole, far, hidden_own, upstream, vectors, bias)
    hidden_far = hidden_sums[:, 0, :half].reshape(-1)
    hidden_near = hidden_sums[:, 0, half:].reshape(-1)
    return (*results, hidden_near, hidden_far)


class Scatter:
    buffers = 8

    def __init__(self, depth, grads, shards, targets, buffers, sems):
        self.depth, self.grads, self.shards, self.targets = depth, grads, shards, targets
        self.held = [buffers[8 * p : 8 * p + 8] for p in range(len(grads))]
        self.me, self.z, self.y, self.x = place()
        self.x_peer = self.z * 4 + self.y * 2 + 1 - self.x
        self.y_peer = self.z * 4 + (1 - self.y) * 2 + self.x
        self.rows = grads[0].shape[0] // (4 * depth)
        (
            self.a1_send, self.a1_recv, self.a2_send, self.a2_recv, self.b2_send, self.b2_recv, self.b1_send, self.b1_recv,
            self.z_send, self.z_recv, self.zc_send, self.zc_recv, self.c_send, self.c_recv, self.out_sem,
        ) = sems

    @staticmethod
    def scratch(depth, rows, classes):
        found = []
        for a, b, c in classes:
            found += [
                pltpu.VMEM((depth, 2 * rows, a), LOW),
                pltpu.VMEM((depth, 2, rows, b), LOW),
                pltpu.VMEM((depth, rows, a), LOW),
                pltpu.VMEM((depth, rows, b), LOW),
                pltpu.VMEM((depth + 1, rows, a + b), LOW),
                pltpu.VMEM((depth + 1, 4 * rows, c), LOW),
                pltpu.VMEM((2 * rows, c), LOW),
                pltpu.VMEM((rows, c), LOW),
            ]
        return found

    @staticmethod
    def semaphores(depth, pieces):
        sem = pltpu.SemaphoreType.DMA
        return [
            *[sem((pieces,)), sem((pieces, depth))] * 3,
            sem((pieces,)),
            sem((pieces, depth, 2)),
            *[sem((pieces,)), sem((pieces, depth + 1))] * 2,
            sem((pieces, 2)),
            sem((pieces, 2)),
            sem((pieces,)),
        ]

    def done(self, p):
        return pltpu.make_async_copy(self.shards[p], self.targets[p], self.out_sem.at[p])

    def columns(self, p):
        a, b, c = (self.held[p][i].shape[-1] for i in (0, 1, 5))
        return pl.ds(0, a), pl.ds(a, b), pl.ds(a + b, c)

    def block(self, zb, yb, xb):
        return zb * 4 + yb * 2 + xb

    def span(self, block, count=1):
        return pl.ds(pl.multiple_of(block * self.rows, self.rows), count * self.rows)

    def add(self, put, count, *terms):
        chunk = min(count, 64)

        @pl.loop(0, count // chunk)
        def _(step):
            at = pl.multiple_of(step * chunk, chunk)
            parts = [term(at, chunk) for term in terms]
            if len(parts) > 2 or put.wide:
                parts = [part.astype(WIDE) for part in parts]
            total = parts[0]
            for part in parts[1:]:
                total = total + part
            put(at, chunk, total)

    def a1(self, p, zb):
        return remote(
            self.grads[p].at[self.span(self.block(zb, 1 - self.y, 0), 2), self.columns(p)[0]],
            self.held[p][0].at[zb],
            self.a1_send.at[p],
            self.a1_recv.at[p, zb],
            self.y_peer,
        )

    def b1(self, p, zb, yb):
        return remote(
            self.grads[p].at[self.span(self.block(zb, yb, 1 - self.x)), self.columns(p)[1]],
            self.held[p][1].at[zb, yb],
            self.b1_send.at[p],
            self.b1_recv.at[p, zb, yb],
            self.x_peer,
        )

    def a2(self, p, zb):
        return remote(
            self.held[p][0].at[zb, self.span(1 - self.x)],
            self.held[p][2].at[zb],
            self.a2_send.at[p],
            self.a2_recv.at[p, zb],
            self.x_peer,
        )

    def b2(self, p, zb):
        return remote(
            self.held[p][1].at[zb, 1 - self.y],
            self.held[p][3].at[zb],
            self.b2_send.at[p],
            self.b2_recv.at[p, zb],
            self.y_peer,
        )

    def slot(self, zb, way):
        return zb if way > 0 else zb + (self.depth - zb) * jnp.where(zb == self.z - 1, 1, 0)

    def z_copy(self, p, zb, way):
        slot = self.slot(zb, way)
        return remote(
            self.held[p][4].at[zb],
            self.held[p][4].at[slot],
            self.z_send.at[p],
            self.z_recv.at[p, slot],
            self.me + 4 * way,
        )

    def zc_copy(self, p, zb, way, first):
        slot = self.slot(zb, way)
        source = self.held[p][5].at[zb]
        if first:
            source = self.grads[p].at[self.span(zb * 4, 4), self.columns(p)[2]]
        return remote(
            source,
            self.held[p][5].at[slot],
            self.zc_send.at[p],
            self.zc_recv.at[p, slot],
            self.me + 4 * way,
        )

    def arrived(self, ref, sem, slot):
        part = ref.at[slot]
        remote(part, part, sem, sem, self.me).wait_recv()

    def cy(self, p):
        return remote(
            self.held[p][5].at[self.z, self.span(2 * (1 - self.y), 2)],
            self.held[p][6],
            self.c_send.at[p, 0],
            self.c_recv.at[p, 0],
            self.y_peer,
        )

    def cx(self, p):
        return remote(
            self.held[p][5].at[self.z, self.span(2 * self.y + 1 - self.x)],
            self.held[p][7],
            self.c_send.at[p, 1],
            self.c_recv.at[p, 1],
            self.x_peer,
        )

    def grad(self, p, block, columns):
        def term(at, count):
            first = pl.multiple_of(block * self.rows + at, 16)
            return self.grads[p][pl.ds(first, count), columns]

        return term

    def part(self, ref, lead, block, columns=None):
        columns = slice(None) if columns is None else columns

        def term(at, count):
            first = pl.multiple_of(block * self.rows + at, 16)
            return ref[(*lead, pl.ds(first, count), columns)]

        return term

    def put(self, ref, lead, block, columns=None):
        columns = slice(None) if columns is None else columns

        def act(at, count, total):
            first = pl.multiple_of(block * self.rows + at, 16)
            ref[(*lead, pl.ds(first, count), columns)] = total.astype(ref.dtype)

        act.wide = ref.dtype == WIDE
        return act

    def open(self, p, zb):
        self.a1(p, zb).start()
        self.b1(p, zb, 0).start()
        self.b1(p, zb, 1).start()

    def first(self, p, zb):
        z, y, x = self.z, self.y, self.x
        a, b, _ = self.columns(p)
        r1a, r1b = self.held[p][0], self.held[p][1]
        self.a1(p, zb).wait_recv()
        self.add(
            self.put(r1a, (zb,), 1 - x),
            self.rows,
            self.part(r1a, (zb,), 1 - x),
            self.grad(p, self.block(zb, y, 1 - x), a),
        )
        self.a2(p, zb).start()
        self.b1(p, zb, 0).wait_recv()
        self.b1(p, zb, 1).wait_recv()
        self.add(
            self.put(r1b, (zb, 1 - y), 0),
            self.rows,
            self.part(r1b, (zb, 1 - y), 0),
            self.grad(p, self.block(zb, 1 - y, x), b),
        )
        self.b2(p, zb).start()

    def terms(self, p, zb):
        z, y, x = self.z, self.y, self.x
        a, b, _ = self.columns(p)
        r1a, r1b, r2a, r2b = self.held[p][:4]
        own = self.block(zb, y, x)
        return (
            [self.grad(p, own, a), self.part(r1a, (zb,), x), self.part(r2a, (zb,), 0)],
            [self.grad(p, own, b), self.part(r1b, (zb, y), 0), self.part(r2b, (zb,), 0)],
        )

    def pass_on(self, p, zb, way):
        a, b, _ = self.columns(p)
        rz = self.held[p][4]
        self.a2(p, zb).wait_recv()
        self.b2(p, zb).wait_recv()
        from_line = (self.z - way >= 0) & (self.z - way < self.depth)

        @pl.when(from_line)
        def _():
            self.arrived(rz, self.z_recv.at[p, zb], zb)
            for terms, columns in zip(self.terms(p, zb), (a, b), strict=True):
                self.add(
                    self.put(rz, (zb,), 0, columns),
                    self.rows,
                    *terms,
                    self.part(rz, (zb,), 0, columns),
                )

        @pl.when(jnp.logical_not(from_line))
        def _():
            for terms, columns in zip(self.terms(p, zb), (a, b), strict=True):
                self.add(self.put(rz, (zb,), 0, columns), self.rows, *terms)

        self.z_copy(p, zb, way).start()

    def pass_c(self, p, zb, way):
        c = self.columns(p)[2]
        rc = self.held[p][5]
        from_line = (self.z - way >= 0) & (self.z - way < self.depth)

        @pl.when(from_line)
        def _():
            self.arrived(rc, self.zc_recv.at[p, zb], zb)
            self.add(
                self.put(rc, (zb,), 0),
                4 * self.rows,
                self.part(rc, (zb,), 0),
                self.grad(p, zb * 4, c),
            )
            self.zc_copy(p, zb, way, False).start()

        @pl.when(jnp.logical_not(from_line))
        def _():
            self.zc_copy(p, zb, way, True).start()

    def own_c(self, p):
        z, depth = self.z, self.depth
        c = self.columns(p)[2]
        rc = self.held[p][5]
        grad = self.grad(p, z * 4, c)
        lower, upper = self.part(rc, (z,), 0), self.part(rc, (depth,), 0)
        put = self.put(rc, (z,), 0)

        @pl.when(z > 0)
        def _():
            self.arrived(rc, self.zc_recv.at[p, z], z)

        @pl.when(z < depth - 1)
        def _():
            self.arrived(rc, self.zc_recv.at[p, depth], depth)

        @pl.when((z > 0) & (z < depth - 1))
        def _():
            self.add(put, 4 * self.rows, grad, lower, upper)

        @pl.when(z == 0)
        def _():
            self.add(put, 4 * self.rows, grad, upper)

        @pl.when(z == depth - 1)
        def _():
            self.add(put, 4 * self.rows, grad, lower)

        self.cy(p).start()

    def turn_c(self, p):
        rc, rcy = self.held[p][5], self.held[p][6]
        self.cy(p).wait_recv()
        self.add(
            self.put(rc, (self.z,), 2 * self.y),
            2 * self.rows,
            self.part(rc, (self.z,), 2 * self.y),
            self.part(rcy, (), 0),
        )
        self.cx(p).start()

    def close(self, p):
        z, depth = self.z, self.depth
        a, b, c = self.columns(p)
        rz, rc, rcx = self.held[p][4], self.held[p][5], self.held[p][7]
        self.a2(p, z).wait_recv()
        self.b2(p, z).wait_recv()

        @pl.when(z > 0)
        def _():
            self.arrived(rz, self.z_recv.at[p, z], z)

        @pl.when(z < depth - 1)
        def _():
            self.arrived(rz, self.z_recv.at[p, depth], depth)

        def total(*slots):
            for terms, columns in zip(self.terms(p, z), (a, b), strict=True):
                lines = [self.part(rz, (slot,), 0, columns) for slot in slots]
                self.add(self.put(self.shards[p], (), 0, columns), self.rows, *terms, *lines)

        pl.when((z > 0) & (z < depth - 1))(lambda: total(z, depth))
        pl.when(z == 0)(lambda: total(depth))
        pl.when(z == depth - 1)(lambda: total(z))
        self.cx(p).wait_recv()
        self.add(
            self.put(self.shards[p], (), 0, c),
            self.rows,
            self.part(rc, (z,), 2 * self.y + self.x),
            self.part(rcx, (), 0),
        )
        self.done(p).start()

    def at_step(self, step, act):
        z, depth = self.z, self.depth
        if step < 0:
            act(z, 0)
            return
        for zb, valid, way in (
            (z + 1 + step, z + 1 + step < depth, 1),
            (z - 1 - step, z - 1 - step >= 0, -1),
        ):
            pl.when(valid)(functools.partial(act, zb, way))

    def stage(self, p, s):
        last = self.depth - 2

        def opened(step):
            self.at_step(step, lambda zb, way: self.open(p, zb))

        def added(step):
            self.at_step(step, lambda zb, way: self.first(p, zb))

        def passed(step):
            self.at_step(step, lambda zb, way: self.pass_on(p, zb, way))

        def passed_c(step):
            self.at_step(step, lambda zb, way: self.pass_c(p, zb, way))

        if s == 0:
            opened(last)
            opened(last - 1)
            passed_c(last)
            return
        if s <= last + 2:
            added(last + 1 - s)
        if last - 1 - s >= -1:
            opened(last - 1 - s)
        if last - s >= 0:
            passed_c(last - s)
        if s >= 2 and last + 2 - s >= 0:
            passed(last + 2 - s)
        if s == last + 1:
            self.own_c(p)
        if s == last + 2:
            self.turn_c(p)
        if s == last + 3:
            self.close(p)

    def sent(self, p):
        passed = pl.ds(0, self.depth - 1)
        for part, sem in (
            (self.held[p][0], self.a1_send),
            (self.held[p][1], self.b1_send),
            (self.held[p][2], self.a2_send),
            (self.held[p][3], self.b2_send),
            (self.held[p][4].at[passed], self.z_send),
            (self.held[p][5].at[passed], self.zc_send),
        ):
            remote(part, part, sem.at[p], sem.at[p], self.me).wait_send()
        self.cy(p).wait_send()
        self.cx(p).wait_send()
        self.done(p).wait()


class SmallSum:
    def __init__(self, lines, buffer, send, recv):
        member = lax.axis_index("tensor")
        self.partners = [{"tensor": 1 - member}, {"dp": lines.x_peer}, {"dp": lines.y_peer}]
        for level in range(lines.depth.bit_length() - 1):
            reach = 1 << level
            way = 1 - 2 * ((lines.z // reach) % 2)
            self.partners.append({"dp": lines.me + 4 * reach * way})
        self.buffer, self.send, self.recv = buffer, send, recv

    def copy(self, step):
        return pltpu.make_async_remote_copy(
            src_ref=self.buffer.at[step],
            dst_ref=self.buffer.at[len(self.partners) + 1 + step],
            send_sem=self.send.at[step],
            recv_sem=self.recv.at[step],
            device_id=self.partners[step],
            device_id_type=MESH,
        )

    def step(self, step):
        if step:
            self.copy(step - 1).wait_recv()
            self.buffer[step] = self.buffer[step - 1] + self.buffer[len(self.partners) + step]
        if step < len(self.partners):
            self.copy(step).start()

    def sent(self):
        for step in range(len(self.partners)):
            self.copy(step).wait_send()


def adamw_update(master, moment, square, gradient, step_rate, decay_rate):
    moment_new = beta_one * moment + (1.0 - beta_one) * gradient
    square_new = beta_two * square + (1.0 - beta_two) * gradient * gradient
    moment_hat = moment_new * (1.0 / (1.0 - beta_one**STEP))
    square_hat = square_new * (1.0 / (1.0 - beta_two**STEP))
    master_new = master - step_rate * (
        moment_hat / (jnp.sqrt(square_hat) + adam_epsilon) + decay_rate * master
    )
    return (moment_new, square_new, master_new)


SCATTER_AT = {
    "reduce": {5: [(0, 0)]},
    "expand": {0: [(0, 1)], 1: [(1, 0)], 5: [(2, 0)], 6: [(0, 2)]},
    "norm": {0: [(1, 1)], 3: [(2, 1)], 4: [(3, 0)]},
    "merge": {1: [(1, 2)]},
    "attend": {1: [(3, 1)], 3: [(0, 3)], 6: [(2, 2)], 7: [(3, 2)], 11: [(2, 3)], 13: [(2, 4)], 14: [(4, 1)], 18: [(3, 4)], 21: [(4, 2)]},
    "project": {0: [(4, 0), (3, 3), (1, 3)], 1: [(5, 0)]},
    "terms": {0: [(4, 3)], 1: [(5, 1)], 2: [(3, 5)], 4: [(0, 4)]},
    "far": {-1: [(5, 2)], 0: [(4, 4)]},
    "near": {0: [(5, 3), (1, 4)]},
    "encoded": {0: [(5, 4), (4, 5)]},
    "end": [(0, 5), (2, 5), (1, 5), (5, 5)],
}


def back_kernel(
    depth, lengths_ref, dealing_ref, vectors_ref,
    whole_ref, far_ref, qkv_in, hidden_turned_in, upstream_in, context_in, totals_in,
    acc_in, normal_in, inverse_in, turned_in, active_in, slope_in, far_ctx_in, *rest,
):
    encoded_out, input_out, small_out, *rest = rest
    targets, rest = rest[:6], rest[6:]
    enc_pair, grad_ref, input_far, acc, arrived, merge_recv, small, score_bias, *rest = rest
    chunk_grads, *rest = rest
    grads, rest = [*[chunk_grads.at[p] for p in range(4)], *rest[:2]], rest[2:]
    shards, rest = rest[:6], rest[6:]
    buffers, rest = rest[: 6 * Scatter.buffers], rest[6 * Scatter.buffers :]
    small_send, small_recv, in_sem, load_sem, ctx_sem, far_send, far_recv, merge_sem, enc_sem, input_sem, *sems = rest
    lines = Scatter(depth, grads, shards, targets, buffers, sems)
    sums = SmallSum(lines, small, small_send, small_recv)
    group = Group(lengths_ref, dealing_ref)
    member = lax.axis_index("tensor")
    rows, width = acc.shape
    total_rows = 2 * rows
    chunks, _, both = active_in.shape
    half = both // 2
    per_piece = chunks // 2
    piece_span = grads[0].shape[1]
    pairs = qkv_in.shape[0]
    inner = pairs * PAIR
    tall, short = 256, 128

    def rows_of(which):
        return pl.ds(pl.multiple_of(which * rows, rows), rows)

    def tile(step, size):
        return pl.ds(pl.multiple_of(step * size, size), size)

    def fetch(source, target, sem):
        return pltpu.make_async_copy(source, target, in_sem.at[sem])

    def phase(name, count, body):
        between = {
            step: [functools.partial(lines.stage, *stage) for stage in stages]
            for step, stages in SCATTER_AT.get(name, {}).items()
        }
        for act in between.pop(-1, ()):
            act()
        looped(count, body, between)

    def places_of(first):
        return first + lax.broadcasted_iota(jnp.int32, (tall, 1), 0)

    def add_sum(row, values):
        small[0, row : row + 1, :] += jnp.sum(values, axis=0, keepdims=True)

    def feed_phase(later, late, late_turned, turned, upstream, active, slope, inner_grad, expand_buf, reduce_buf, leaving):
        def active_load(j):
            slot = lax.rem(j, 2)
            return [pltpu.make_async_copy(active_in.at[j], active.at[slot], load_sem.at[slot, 4])]

        def loads(j):
            slot = lax.rem(j, 2)
            array, *firsts = chunk_columns(j, per_piece, half)
            copies = [pltpu.make_async_copy(slope_in.at[j], slope.at[slot], load_sem.at[slot, 5])]
            for kind, buf in enumerate((expand_buf, reduce_buf)):
                first = pl.multiple_of(firsts[kind], half)
                for side, source in enumerate((far_ref, whole_ref)):
                    copies.append(
                        pltpu.make_async_copy(
                            source.at[array, :, pl.ds(first, half)],
                            buf.at[slot, :, pl.ds(side * half, half)],
                            load_sem.at[slot, 2 * kind + side],
                        )
                    )
            return copies

        def taken(j, load):
            for copy in load(j):
                copy.wait()

            @pl.when(j + 1 < chunks)
            def _():
                for copy in load(j + 1):
                    copy.start()

        acc_copy = fetch(acc_in, acc, 0)
        acc_copy.start()
        fetches = [fetch(upstream_in, upstream, 1), fetch(turned_in, turned, 2)]
        for copy in fetches:
            copy.start()
        for copy in [*active_load(0), *loads(0)]:
            copy.start()
        greet_line(
            lines.me, lines.z, lines.y, lines.x, depth, [sums.partners[0], *sums.partners[3:]]
        )
        for copy in later:
            copy.start()
        small[0] = jnp.zeros(small.shape[1:], WIDE)
        score_bias[...] = group.score_bias(total_rows - LONGEST)
        acc_copy.wait()
        for copy in fetches:
            copy.wait()

        def late_tile(step):
            at = tile(step, short)
            unit, scale = norm(acc[at, :])
            upper = upstream[at, :].astype(WIDE)
            upstream[at, :] = (unit * vectors_ref[6:7, :] + vectors_ref[7:8, :]).astype(LOW)
            add_sum(6, upper * unit)
            add_sum(7, upper)
            grad = norm_back(upper * vectors_ref[6:7, :], unit, scale)
            grad_low = grad.astype(LOW)
            add_sum(5, grad_low.astype(WIDE))
            acc[at, :] = grad
            late[at, :] = grad_low
            late_turned[:, at] = grad.T.astype(LOW)

        looped(rows // short, late_tile, {})
        enc_near = pltpu.make_async_copy(upstream, enc_pair.at[member], enc_sem.at[2])
        enc_far = other_core(upstream, enc_pair.at[member], enc_sem.at[0], enc_sem.at[1])
        enc_near.start()
        enc_far.start()

        def send(k):
            slot = lax.rem(k, 2)
            return other_core(
                leaving.at[slot], arrived.at[slot], far_send.at[slot], far_recv.at[slot]
            )

        def own_columns(k):
            return pl.ds(pl.multiple_of(lax.rem(k, per_piece) * half, half), half)

        def finish(k):
            piece, slot = k // per_piece, lax.rem(k, 2)
            send(k).wait_recv()

            @pl.loop(0, width // tall)
            def _(step):
                at = tile(step, tall)
                chunk_grads[piece, at, own_columns(k)] += arrived[slot, at, :]

        def products(k, left, right):
            piece, slot = k // per_piece, lax.rem(k, 2)

            @pl.when(k >= 2)
            def _():
                send(k - 2).wait_send()

            parts = [
                dot_nn(left[step * tall : (step + 1) * tall, :], right[...])
                for step in range(width // tall)
            ]
            for step, part in enumerate(parts):
                at = slice(step * tall, (step + 1) * tall)
                leaving[slot, at, :] = part[:, 0:half].astype(LOW)
                chunk_grads[piece, at, own_columns(k)] = part[:, half:both].astype(LOW)

            @pl.when(k >= 1)
            def _():
                finish(k - 1)

            send(k).start()

        def reduce_chunk(j):
            taken(j, active_load)
            products(j, late_turned, active.at[lax.rem(j, 2)])

        def expand_chunk(j):
            slot = lax.rem(j, 2)
            taken(j, loads)
            total = jnp.zeros((1, both), WIDE)
            tiles = [slice(step * tall, (step + 1) * tall) for step in range(rows // tall)]
            parts = [dot_nn(late[at, :], reduce_buf[slot]) for at in tiles]
            for at, part in zip(tiles, parts, strict=True):
                grad = (part * slope[slot, at, :].astype(WIDE)).astype(LOW)
                inner_grad[at, :] = grad
                total = total + jnp.sum(grad.astype(WIDE), axis=0, keepdims=True)
                acc[at, :] += dot_nt(grad, expand_buf[slot])
            for which, side in ((1 - member, 0), (member, half)):
                row = 8 + which * 2 + j // per_piece
                small[0, pl.ds(row, 1), own_columns(j)] = total[:, side : side + half]
            products(chunks + j, turned, inner_grad)

        phase("reduce", chunks, reduce_chunk)
        phase("expand", chunks, expand_chunk)
        finish(2 * chunks - 1)
        for k in (2 * chunks - 2, 2 * chunks - 1):
            send(k).wait_send()
        enc_near.wait()
        enc_far.wait()

    def merge_phase(normal, inverse, near_ctx, far_ctx, merge, merge_far, fetches, turned, grad_own, grad_far, merge_send):
        for copy in fetches:
            copy.wait()

        def norm_tile(step):
            at = tile(step, short)
            grad = acc[at, :]
            unit = normal[at, :]
            add_sum(3, grad * unit)
            add_sum(4, grad)
            branch_grad = norm_back(grad * vectors_ref[3:4, :], unit, inverse[at, 0:1])
            branch_low = branch_grad.astype(LOW)
            add_sum(2, branch_low.astype(WIDE))
            acc[at, :] = branch_grad
            turned[:, at] = branch_grad.T.astype(LOW)
            grad_far[at, :] = dot_nn(branch_low, merge_far[...]).astype(LOW)
            grad_own[at, :] = dot_nn(branch_low, merge[...]).astype(LOW)

        phase("norm", rows // short, norm_tile)
        out_grad = other_core(grad_far, grad_ref.at[rows_of(member)], ctx_sem.at[0], ctx_sem.at[1])
        in_grad = pltpu.make_async_copy(grad_own, grad_ref.at[rows_of(member)], ctx_sem.at[2])
        out_grad.start()
        in_grad.start()
        out_merge = other_core(merge_send, merge_recv, merge_sem.at[0], merge_sem.at[1])

        def merge_step(which):
            @pl.when(which == 0)
            def _():
                for step in range(width // tall):
                    at = slice(step * tall, (step + 1) * tall)
                    merge_send[at, :] = dot_nn(turned[at, :], far_ctx[...]).astype(LOW)
                out_merge.start()

            @pl.when(which == 1)
            def _():
                out_merge.wait()
                for step in range(width // tall):
                    at = slice(step * tall, (step + 1) * tall)
                    grads[4][at, 0:inner] = (
                        dot_nn(turned[at, :], near_ctx[...]) + merge_recv[at, :].astype(WIDE)
                    ).astype(LOW)

        phase("merge", 2, merge_step)
        out_grad.wait()
        in_grad.wait()

    def early_phase(normal, inverse, near_ctx, far_ctx, merge, merge_far):
        merge_columns = pl.ds(whole_ref.shape[2] - inner, inner)
        fetches = [
            fetch(normal_in, normal, 3),
            fetch(inverse_in, inverse, 4),
            fetch(context_in.at[rows_of(member)], near_ctx, 5),
            fetch(far_ctx_in, far_ctx, 6),
            fetch(whole_ref.at[0, :, merge_columns], merge, 7),
            fetch(far_ref.at[0, :, merge_columns], merge_far, 8),
        ]
        pl.run_scoped(
            functools.partial(feed_phase, fetches),
            pltpu.VMEM((rows, width), LOW),
            pltpu.VMEM((width, rows), LOW),
            pltpu.VMEM((width, rows), LOW),
            pltpu.VMEM((rows, width), LOW),
            pltpu.VMEM((2, rows, both), LOW),
            pltpu.VMEM((2, rows, both), LOW),
            pltpu.VMEM((rows, both), LOW),
            pltpu.VMEM((2, width, both), LOW),
            pltpu.VMEM((2, width, both), LOW),
            pltpu.VMEM((2, width, half), LOW),
        )
        pl.run_scoped(
            functools.partial(
                merge_phase, normal, inverse, near_ctx, far_ctx, merge, merge_far, fetches
            ),
            pltpu.VMEM((width, rows), LOW),
            pltpu.VMEM((rows, inner), LOW),
            pltpu.VMEM((rows, inner), LOW),
            pltpu.VMEM((width, inner), LOW),
        )

    pl.run_scoped(
        early_phase,
        pltpu.VMEM((rows, width), WIDE),
        pltpu.VMEM((rows, 128), WIDE),
        pltpu.VMEM((rows, inner), LOW),
        pltpu.VMEM((rows, inner), LOW),
        pltpu.VMEM((width, inner), LOW),
        pltpu.VMEM((width, inner), LOW),
    )

    def last_phase(mixed):
        def attend_phase(qkv, context, upper, totals, dots, key_turned, queries, uppers, query_sum, hidden_turned):
            def loads(pair, slot):
                columns = pl.ds(pl.multiple_of(pair * PAIR, PAIR), PAIR)
                return [
                    pltpu.make_async_copy(qkv_in.at[pair], qkv.at[slot], load_sem.at[slot, 0]),
                    pltpu.make_async_copy(
                        context_in.at[:, columns], context.at[slot], load_sem.at[slot, 1]
                    ),
                    pltpu.make_async_copy(
                        grad_ref.at[:, columns], upper.at[slot], load_sem.at[slot, 2]
                    ),
                ]

            fetches = [fetch(totals_in, totals, 0)]
            for copy in [*loads(0, 0), *fetches]:
                copy.start()
            for copy in fetches:
                copy.wait()
            blocks = ((0, LONGEST), (LONGEST, total_rows - LONGEST))
            per_pair = total_rows // TILE

            def hidden_tile(step, slot):
                return pltpu.make_async_copy(
                    hidden_turned_in.at[tile(step, tall), :],
                    hidden_turned.at[slot],
                    load_sem.at[slot, 3],
                )

            def project(second):
                grad, first = (grads[5], 0) if second else (grads[4], inner)
                span = (pairs // 2) * 3 * PAIR
                columns = slice(span if second else 0, span * 2 if second else span)
                hidden_tile(0, 0).start()
                for step in range(width // tall):
                    if step + 1 < width // tall:
                        hidden_tile(step + 1, (step + 1) % 2).start()
                    hidden_tile(step, step % 2).wait()
                    grad[step * tall : (step + 1) * tall, first : first + span] = dot_nn(
                        hidden_turned[step % 2], mixed[:, columns]
                    ).astype(LOW)

            def pair_body(pair):
                slot = lax.rem(pair, 2)
                for copy in loads(pair, slot):
                    copy.wait()

                @pl.when(pair + 1 < pairs)
                def _():
                    for copy in loads(pair + 1, 1 - slot):
                        copy.start()

                attend_back_open(
                    qkv.at[slot], context.at[slot], upper.at[slot], dots, key_turned, queries, uppers
                )
                base = pair * 3 * PAIR

                def columns(which):
                    return pl.ds(pl.multiple_of(base + which * PAIR, PAIR), PAIR)

                for begin, size in blocks:
                    block = slice(begin, begin + size)
                    query_sum[:, block] = jnp.zeros((PAIR, size), WIDE)

                    def key_tile(step, begin=begin, size=size):
                        at, key_sum, value_sum = attend_back_tile(
                            qkv.at[slot], score_bias, totals.at[pair], dots, key_turned, queries, uppers, query_sum,
                            begin, size, step,
                        )
                        mixed[at, columns(1)] = key_sum.astype(LOW)
                        mixed[at, columns(2)] = value_sum.astype(LOW)

                    between = {}
                    for step in range(size // TILE):
                        number = begin // TILE + step
                        for act_pair in range(pairs):
                            for p, s in SCATTER_AT["attend"].get(act_pair * per_pair + number, ()):

                                def act(act_pair=act_pair, p=p, s=s):
                                    pl.when(pair == act_pair)(lambda: lines.stage(p, s))

                                between.setdefault(step, []).append(act)
                    looped(size // TILE, key_tile, between)
                    mixed[block, columns(0)] = (
                        (query_sum[:, block] * HEAD_DIM ** (-0.5)).T.astype(LOW)
                    )
                for which, row in ((0, 0), (2, 1)):
                    part = mixed[:, columns(which)].astype(WIDE)
                    spot = pl.multiple_of(member * inner + pair * PAIR, PAIR)
                    small[0, row : row + 1, pl.ds(spot, PAIR)] = jnp.sum(
                        part, axis=0, keepdims=True
                    )

            def project_stages(second):
                return [
                    functools.partial(project, second),
                    *[functools.partial(lines.stage, *st) for st in SCATTER_AT["project"][second]],
                ]

            looped(pairs, pair_body, {1: project_stages(0), 3: project_stages(1)})

        pl.run_scoped(
            attend_phase,
            pltpu.VMEM((2, total_rows, 3 * PAIR), LOW),
            pltpu.VMEM((2, total_rows, PAIR), LOW),
            pltpu.VMEM((2, total_rows, PAIR), LOW),
            pltpu.VMEM(totals_in.shape, WIDE),
            pltpu.VMEM((8, total_rows), WIDE),
            pltpu.VMEM((PAIR, total_rows), LOW),
            pltpu.VMEM((2, total_rows, PAIR), LOW),
            pltpu.VMEM((2, total_rows, PAIR), LOW),
            pltpu.VMEM((PAIR, total_rows), WIDE),
            pltpu.VMEM((2, tall, total_rows), LOW),
        )
        sums.step(0)

        def input_phase(weight, terms, leaving, pair):
            weight_copy = fetch(whole_ref.at[0, :, pl.ds(0, pairs * 3 * PAIR)], weight, 0)
            weight_copy.start()
            pair_copies = [fetch(enc_pair.at[i], pair.at[rows_of(i)], 3 + i) for i in range(2)]
            for copy in pair_copies:
                copy.start()
            weight_copy.wait()

            def term_tile(step):
                at = tile(step, tall)
                total = dot_nt(mixed[at, :], weight[...])
                own = rows // tall
                mine = step // own == member

                @pl.when(mine)
                def _():
                    terms[at, :] = (total + acc[tile(lax.rem(step, own), tall), :]).astype(LOW)

                @pl.when(jnp.logical_not(mine))
                def _():
                    terms[at, :] = total.astype(LOW)

            phase("terms", total_rows // tall, term_tile)
            sums.step(1)

            def own_rows(which, step):
                places = places_of(which * rows + step * tall)
                return picked_rows(group.moved(places, group.own, group.first), terms)

            def far_tile(step):
                leaving[tile(step, tall), :] = own_rows(1 - member, step).astype(LOW)

            phase("far", rows // tall, far_tile)
            crossing = other_core(leaving, input_far, input_sem.at[0], input_sem.at[1])
            crossing.start()
            sums.step(2)

            def near_tile(step):
                acc[tile(step, tall), :] = own_rows(member, step)

            phase("near", rows // tall, near_tile)
            sums.step(3)
            crossing.wait()
            back = fetch(input_far, leaving, 2)
            back.start()
            back.wait()

            @pl.loop(0, rows // short)
            def _(step):
                at = tile(step, short)
                leaving[at, :] = (acc[at, :] + leaving[at, :].astype(WIDE)).astype(LOW)

            done = fetch(leaving, input_out, 2)
            done.start()
            for copy in pair_copies:
                copy.wait()

            def encoded_tile(step):
                places = places_of(member * rows + step * tall)
                index = group.moved(places, group.dealt, group.first)
                terms[tile(step, tall), :] = picked_rows(index, pair).astype(LOW)

            phase("encoded", rows // tall, encoded_tile)
            done.wait()
            done = fetch(terms.at[pl.ds(0, rows)], encoded_out, 2)
            done.start()
            done.wait()

        pl.run_scoped(
            input_phase,
            pltpu.VMEM((width, pairs * 3 * PAIR), LOW),
            pltpu.VMEM((total_rows, width), LOW),
            pltpu.VMEM((rows, width), LOW),
            pltpu.VMEM((total_rows, width), LOW),
        )

    pl.run_scoped(last_phase, pltpu.VMEM((total_rows, pairs * 3 * PAIR), LOW))

    for step in range(4, len(sums.partners) + 1):
        sums.step(step)
    small_out[...] = small[len(sums.partners)]
    for st in SCATTER_AT["end"]:
        lines.stage(*st)
    sums.sent()
    for p in range(len(grads)):
        lines.sent(p)


def finish_kernel(*refs):
    sources, refs = refs[:27], refs[27:]
    targets, refs = refs[:21], refs[21:]
    held, made, (in_sem, out_sem) = refs[:27], refs[27:46], refs[46:]
    loads = [pltpu.make_async_copy(sources[i], held[i], in_sem.at[i]) for i in range(27)]
    for copy in loads:
        copy.start()
    small_ref, *smalls = held[:7]
    vectors_ref, vectors_first, vectors_second, hidden_ref, hidden_first, hidden_second = smalls
    shards, ins, rows_held = held[7:13], held[13:25], held[25:]
    vector_grad_ref, *rest = made
    outs, small_out = rest[:12], rest[12:]
    results = [*rows_held, *made]
    writes = [pltpu.make_async_copy(results[i], targets[i], out_sem.at[i]) for i in range(21)]
    for copy in loads[:7]:
        copy.wait()
    width = vectors_ref.shape[1]
    inner = ins[3].shape[1]
    pairs = inner // PAIR
    span = shards[0].shape[1]
    vector_grad_ref[...] = small_ref[0:8, :]
    states = vectors_ref[...], vectors_first[...], vectors_second[...]
    for i, value in enumerate(adamw_update(*states, small_ref[0:8, :], rate_vectors, 0.0)):
        small_out[i][...] = value
    for i in range(hidden_ref.shape[1] // width):
        columns = slice(i * width, (i + 1) * width)
        states = hidden_ref[:, columns], hidden_first[:, columns], hidden_second[:, columns]
        grad = small_ref[8 + i : 9 + i, :]
        for n, value in enumerate(adamw_update(*states, grad, rate_hidden, 0.0)):
            small_out[3 + n][:, columns] = value

    def update(matrix, lead, columns, grad, grad_columns):
        rate = (rate_project, rate_merge, rate_expand, rate_reduce)[matrix]

        @pl.loop(0, grad.shape[0] // 16)
        def _(step):
            at = pl.ds(pl.multiple_of(step * 16, 16), 16)
            old = [ins[3 * matrix + i][(*lead, at, columns)] for i in range(3)]
            new = adamw_update(*old, grad[at, grad_columns], rate, weight_decay)
            for i in range(3):
                outs[3 * matrix + i][(*lead, at, columns)] = new[i]

    for i in (2, *range(15, 21)):
        writes[i].start()
    for copy in loads[7:13]:
        copy.wait()
    for matrix in (3, 2, 1, 0):
        for copy in loads[13 + 3 * matrix : 16 + 3 * matrix]:
            copy.wait()
        if matrix >= 2:
            for i in range(2):
                columns = slice(i * span, (i + 1) * span)
                update(matrix, (), columns, shards[2 * (3 - matrix) + i], slice(0, span))
        elif matrix == 1:
            update(matrix, (), slice(0, inner), shards[4], slice(0, inner))
        else:
            for pair in range(pairs):
                piece, begin = (4, inner) if pair < pairs // 2 else (5, 0)
                for c in range(3):
                    at = begin + (3 * (pair % (pairs // 2)) + c) * PAIR
                    columns = slice(pair * PAIR, (pair + 1) * PAIR)
                    update(matrix, (c,), columns, shards[piece], slice(at, at + PAIR))
        for copy in writes[3 + 3 * matrix : 6 + 3 * matrix]:
            copy.start()
        if matrix == 3:
            for copy in loads[25:]:
                copy.wait()
            for copy in writes[:2]:
                copy.start()
    for copy in writes:
        copy.wait()


def finish(small, shards, rows_out, matrices, vectors, hidden):
    states = [one for matrix in matrices for one in matrix]
    operands = [small, *vectors, *hidden, *shards, *states, *rows_out]
    shape, sem = jax.ShapeDtypeStruct, pltpu.SemaphoreType.DMA
    results = [
        *[shape(one.shape, LOW) for one in rows_out],
        shape((8, small.shape[1]), WIDE),
        *[shape(one.shape, WIDE) for one in (*states, *vectors, *hidden)],
    ]
    anywhere = pl.BlockSpec(memory_space=pl.ANY)
    return pl.pallas_call(
        finish_kernel,
        in_specs=[anywhere] * len(operands),
        out_specs=[anywhere] * len(results),
        out_shape=results,
        scratch_shapes=[
            *[pltpu.VMEM(one.shape, one.dtype) for one in operands],
            *[pltpu.VMEM(one.shape, one.dtype) for one in results[2:]],
            sem((len(operands),)),
            sem((len(results),)),
        ],
        compiler_params=pltpu.CompilerParams(vmem_limit_bytes=63 * MIB),
    )(*operands)


def back(lengths, dealing, vectors, whole, far, kept, parts):
    qkv, hidden_turned, upstream, context, totals, acc, *_ = kept
    rows, width = acc.shape
    total_rows, inner = context.shape
    depth, shard_rows = parts // 4, width // parts
    half, pair_span = 256, 3 * PAIR * (qkv.shape[0] // 2)
    piece_span = whole.shape[2] // 2
    spans = (*[piece_span] * 4, inner + pair_span, pair_span)
    classes = []
    for span in spans:
        third = max(128, span // 5 // 128 * 128)
        if (span - third) % 256:
            third += 128
        classes.append(((span - third) // 2, (span - third) // 2, third))
    shape, sem = jax.ShapeDtypeStruct, pltpu.SemaphoreType.DMA
    vmem, anywhere = pl.BlockSpec(memory_space=pltpu.VMEM), pl.BlockSpec(memory_space=pl.ANY)
    steps = 3 + depth.bit_length() - 1
    results = pl.pallas_call(
        functools.partial(back_kernel, depth),
        in_specs=[
            *[pl.BlockSpec(memory_space=pltpu.SMEM)] * 2,
            vmem,
            *[anywhere] * (2 + len(kept)),
        ],
        out_specs=[*[anywhere] * 2, vmem, *[anywhere] * (len(spans) + 3)],
        out_shape=[
            shape((rows, width), LOW),
            shape((rows, width), LOW),
            shape((16, width), WIDE),
            *[shape((shard_rows, span), WIDE) for span in spans],
            shape((2, rows, width), LOW),
            shape((total_rows, inner), LOW),
            shape((rows, width), LOW),
        ],
        scratch_shapes=[
            pltpu.VMEM((rows, width), WIDE),
            pltpu.VMEM((2, width, half), LOW),
            pltpu.VMEM((width, inner), LOW),
            pltpu.VMEM((2 * steps + 1, 16, width), WIDE),
            pltpu.VMEM((total_rows - LONGEST, total_rows - LONGEST), WIDE),
            pltpu.VMEM((4, width, piece_span), LOW),
            *[pltpu.VMEM((width, span), LOW) for span in spans[4:]],
            *[pltpu.VMEM((shard_rows, span), WIDE) for span in spans],
            *Scatter.scratch(depth, shard_rows, classes),
            sem((steps,)),
            sem((steps,)),
            sem((9,)),
            sem((2, 6)),
            sem((3,)),
            sem((2,)),
            sem((2,)),
            sem((2,)),
            sem((3,)),
            sem((2,)),
            *Scatter.semaphores(depth, len(spans)),
        ],
        compiler_params=pltpu.CompilerParams(
            collective_id=1, has_side_effects=True, vmem_limit_bytes=63 * MIB
        ),
    )(lengths, dealing, vectors, whole, far, *kept)
    return results[:2], results[2], results[3 : 3 + len(spans)]


def by_kernels(tokens, cotangent, lengths, dealing, project, merge, expand, reduce, vectors, hidden, parts):
    hidden = tuple(one.reshape(1, -1) for one in hidden)
    matrices = (project, merge, expand, reduce)
    whole, far, *kept = front(
        lengths, dealing, *[one[0] for one in matrices], vectors[0], hidden[0], tokens, cotangent, parts
    )
    rows_out, small, shards = back(lengths, dealing, vectors[0], whole, far, kept, parts)
    results = finish(small, shards, rows_out, matrices, vectors, hidden)
    encoded, input_grad, vector_grad = results[:3]
    news = [results[3 + 3 * i : 6 + 3 * i] for i in range(6)]
    return (
        encoded,
        input_grad,
        *news[0],
        *[one.T for one in news[1]],
        *news[2],
        *[one.T for one in news[3]],
        *news[4],
        *[one.reshape(-1) for one in news[5]],
        vector_grad,
    )


def local(
    tokens,
    cotangent,
    lengths,
    dealing,
    project_weight,
    project_first,
    project_second,
    merge_weight,
    merge_first,
    merge_second,
    expand_weight,
    expand_first,
    expand_second,
    reduce_weight,
    reduce_first,
    reduce_second,
    vectors,
    vector_first,
    vector_second,
    hidden_bias,
    hidden_first,
    hidden_second,
):
    parts = lax.axis_size("dp")
    member = lax.axis_index("tensor")
    other = 1 - member
    half_rows, model_width = tokens.shape
    total_rows = 2 * half_rows
    width_half = project_weight.shape[2]
    pairs = width_half // PAIR
    hidden_half = expand_weight.shape[1]
    shard_rows = expand_weight.shape[0]
    own_begin = member * half_rows
    by_kernel = parts % 4 == 0 and (parts & (parts - 1)) == 0 and shard_rows % 16 == 0

    def swap(value):
        return lax.ppermute(value, "tensor", [(0, 1), (1, 0)])

    def own(value, size, which=member):
        return lax.dynamic_slice_in_dim(value, which * size, size, 0)

    if by_kernel:
        return by_kernels(
            tokens, cotangent, lengths, dealing,
            (project_weight, project_first, project_second),
            (merge_weight.T, merge_first.T, merge_second.T),
            (expand_weight, expand_first, expand_second),
            (reduce_weight.T, reduce_first.T, reduce_second.T),
            (vectors, vector_first, vector_second),
            (hidden_bias, hidden_first, hidden_second),
            parts,
        )

    segment, own_of, dealt_of, from_own, from_dealt = layout(lengths[0], dealing[0], total_rows)
    dealt_of = own(dealt_of, half_rows)
    short = segment[LONGEST:]
    score_bias = jnp.where(short[:, None] == short[None, :], 0.0, masked_score).astype(WIDE)

    def own_first(index):
        return lax.rem(index - own_begin + total_rows, total_rows)

    projections = (
        project_weight.reshape(3, shard_rows, pairs, PAIR)
        .transpose(1, 2, 0, 3)
        .reshape(shard_rows, 3 * width_half)
    )
    quarter = hidden_half // 2
    reduce_turned = reduce_weight.T
    shards = jnp.stack(
        [
            jnp.concatenate([projections, merge_weight.T], axis=1),
            jnp.concatenate([expand_weight[:, :quarter], reduce_turned[:, :quarter]], axis=1),
            jnp.concatenate([expand_weight[:, quarter:], reduce_turned[:, quarter:]], axis=1),
        ]
    ).astype(LOW)
    zeros_pair = jnp.zeros((pairs, PAIR), WIDE)
    bias_row = jnp.concatenate(
        [
            own(vectors[0], width_half).reshape(pairs, PAIR),
            zeros_pair,
            own(vectors[1], width_half).reshape(pairs, PAIR),
        ],
        axis=1,
    ).reshape(pairs, 1, 3 * PAIR)
    whole = lax.all_gather(shards, "dp", axis=1, tiled=True)
    far = swap(whole)
    token_pair = jnp.concatenate([tokens, swap(tokens)], axis=0)
    upper_pair = jnp.concatenate([cotangent, swap(cotangent)], axis=0)
    hidden = dot_nn(pick_rows(own_first(own_of), total_rows), token_pair).astype(LOW)
    upstream = dot_nn(pick_rows(own_first(dealt_of), total_rows), upper_pair).astype(LOW)
    qkv = jnp.einsum(
        "rd,dpc->prc",
        hidden,
        whole[0, :, : 3 * width_half].reshape(model_width, pairs, 3 * PAIR),
        preferred_element_type=WIDE,
    )
    qkv = (qkv + bias_row).astype(LOW)
    context, totals = attend(qkv, score_bias)

    (
        encoded, branch_grad, context_grad, merge_grad, expand_grad, reduce_grad, sums, hidden_part_own, hidden_part_far,
    ) = feed_block(
        context,
        whole,
        far,
        own(hidden, half_rows),
        upstream,
        vectors,
        own(hidden_bias, hidden_half),
        own(hidden_bias, hidden_half, other),
    )
    encoded_pair = jnp.concatenate([encoded, swap(encoded)], axis=0)
    encoded_out = dot_nn(
        pick_rows(own_first(own(from_dealt, half_rows)), total_rows), encoded_pair
    ).astype(LOW)
    mixed_grads = attend_back(qkv, score_bias, context, context_grad, totals)
    mixed_sums = jnp.sum(mixed_grads.astype(WIDE), axis=1).reshape(pairs, 3, PAIR)
    mixed_grads = mixed_grads.transpose(1, 0, 2).reshape(total_rows, 3 * width_half)
    project_grad = dot_tn(hidden, mixed_grads)
    input_terms = dot_nt(mixed_grads, whole[0, :, : 3 * width_half])
    own_part = own(input_terms, half_rows) + branch_grad
    input_terms = lax.dynamic_update_slice_in_dim(input_terms, own_part, own_begin, 0).astype(LOW)
    input_far = swap(
        dot_nn(pick_rows(own(from_own, half_rows, other), total_rows), input_terms).astype(LOW)
    )
    input_grad = (
        dot_nn(pick_rows(own(from_own, half_rows), total_rows), input_terms)
        + input_far.astype(WIDE)
    ).astype(LOW)
    zeros_width = jnp.zeros((model_width,), WIDE)
    zeros_hidden = jnp.zeros_like(hidden_bias)
    hidden_total = lax.dynamic_update_slice_in_dim(
        lax.dynamic_update_slice_in_dim(
            zeros_hidden, hidden_part_own, member * hidden_half, 0
        ),
        hidden_part_far,
        other * hidden_half,
        0,
    )
    vector_rows = [
        lax.dynamic_update_slice_in_dim(
            zeros_width, mixed_sums[:, c].reshape(-1), member * width_half, 0
        )
        for c in (0, 2)
    ]
    small = jnp.concatenate(
        [
            jnp.stack(vector_rows),
            sums[2:],
            hidden_total.reshape(-1, model_width),
            jnp.zeros((4, model_width), WIDE),
        ],
        axis=0,
    )
    grads = [
        lax.psum_scatter(g.astype(LOW), "dp", scatter_dimension=0, tiled=True).astype(WIDE)
        for g in (project_grad, merge_grad, expand_grad, reduce_grad)
    ]
    small = lax.psum(small, ("dp", "tensor"))
    project_shard, merge_shard, expand_shard, reduce_shard = grads
    project_shard = (
        project_shard.reshape(shard_rows, pairs, 3, PAIR)
        .transpose(2, 0, 1, 3)
        .reshape(3, shard_rows, width_half)
    )
    vector_grad = small[:8]
    hidden_grad = small[8:12].reshape(-1)
    return (
        encoded_out,
        input_grad,
        *adamw_update(
            project_weight, project_first, project_second, project_shard, rate_project, weight_decay
        ),
        *adamw_update(
            merge_weight, merge_first, merge_second, merge_shard.T, rate_merge, weight_decay
        ),
        *adamw_update(
            expand_weight, expand_first, expand_second, expand_shard, rate_expand, weight_decay
        ),
        *adamw_update(
            reduce_weight, reduce_first, reduce_second, reduce_shard.T, rate_reduce, weight_decay
        ),
        *adamw_update(vectors, vector_first, vector_second, vector_grad, rate_vectors, 0.0),
        *adamw_update(hidden_bias, hidden_first, hidden_second, hidden_grad, rate_hidden, 0.0),
        vector_grad,
    )


def solution(mesh):
    sharded = (
        P("dp", None),
        P("dp", None),
        *[P(None, "dp", "tensor")] * 3,
        *[P("tensor", "dp")] * 3,
        *[P("dp", "tensor")] * 3,
        *[P("tensor", "dp")] * 3,
        *[P()] * 6,
    )
    rows = P(("dp", "tensor"), None)
    return jax.shard_map(
        local,
        mesh=mesh,
        in_specs=(rows, rows, *sharded),
        out_specs=(rows, rows, *sharded[2:], P()),
        check_vma=False,
    )
```

profile of v0, /device:TPU:0, one launch (start us, length us, event | category | flops | bytes accessed | tf_op | source)
XLA Modules:
  0.0 290.8 jit_solution(16890921345145833681)
XLA Ops:
  0.7 130.6 %shard_map.373 = (bf16[3,1024,2048]{2,1,0:T(8,128)(2,1)}, bf16[3,1024,2048]{2,1,0:T(8,128)(2,1)}, bf16[4,1536,384]{2,1,0:T(8,128)(2,1)}, bf16[1024,1536]{1,0:T(8...) custom-call(s32[1,4]{1,0:T(1,128)} %lengths_ref.3, ...), custom_call_target="tpu_custom_call" | custom-call | tf_op jit(solution)/shard_map/pallas_call | solution.py:891
  131.3 151.9 %shard_map.374 = (bf16[768,1024]{1,0:T(8,128)(2,1)}, bf16[768,1024]{1,0:T(8,128)(2,1)}, f32[16,1024]{1,0:T(8,128)}, f32[64,1024]{1,0:T(8,128)}, f32[64,1024]{1,0...) custom-call(s32[1,4]{1,0:T(1,128)} %lengths_ref.3, ...), custom_call_target="tpu_custom_call" | custom-call | tf_op jit(solution)/shard_map/pallas_call | solution.py:2319
  283.2 7.4 %shard_map.375 = (bf16[768,1024]{1,0:T(8,128)(2,1)}, bf16[768,1024]{1,0:T(8,128)(2,1)}, f32[8,1024]{1,0:T(8,128)}, f32[3,64,512]{2,1,0:T(8,128)}, f32[3,64,512]{...) custom-call(f32[16,1024]{1,0:T(8,128)} %get-tuple-element.79.refs_0_, ...), custom_call_target="tpu_custom_call" | custom-call | tf_op jit(solution)/shard_map/pallas_call | solution.py:2287
where the time goes:
time: 295 us; the launch traced here: 291 us
  Pallas kernels  290 us (98%)
    pallas_call x1, Pallas kernels, back(): pl.pallas_call(functools.partial(back_kernel, depth), in_specs=[*[pl.Bloc...  152 us
    pallas_call x1, Pallas kernels, front(): pl.pallas_call(functools.partial(front_kernel, depth), in_specs=[*[pl.Blo...  131 us
    pallas_call x1, Pallas kernels, finish(): pl.pallas_call(finish_kernel, in_specs=[anywhere] * len(operands), out_sp...  7.41 us

commit v1 on v0

--- a/solution.py
+++ b/solution.py
@@ -1707,17 +1707,16 @@
 
 
 SCATTER_AT = {
-    "reduce": {5: [(0, 0)]},
-    "expand": {0: [(0, 1)], 1: [(1, 0)], 5: [(2, 0)], 6: [(0, 2)]},
-    "norm": {0: [(1, 1)], 3: [(2, 1)], 4: [(3, 0)]},
-    "merge": {1: [(1, 2)]},
-    "attend": {1: [(3, 1)], 3: [(0, 3)], 6: [(2, 2)], 7: [(3, 2)], 11: [(2, 3)], 13: [(2, 4)], 14: [(4, 1)], 18: [(3, 4)], 21: [(4, 2)]},
-    "project": {0: [(4, 0), (3, 3), (1, 3)], 1: [(5, 0)]},
-    "terms": {0: [(4, 3)], 1: [(5, 1)], 2: [(3, 5)], 4: [(0, 4)]},
-    "far": {-1: [(5, 2)], 0: [(4, 4)]},
-    "near": {0: [(5, 3), (1, 4)]},
-    "encoded": {0: [(5, 4), (4, 5)]},
-    "end": [(0, 5), (2, 5), (1, 5), (5, 5)],
+    "expand": {0: [(0, 0)], 3: [(0, 1)], 5: [(0, 2)]},
+    "norm": {-1: [(1, 0)]},
+    "merge": {1: [(0, 3)]},
+    "attend": {1: [(1, 1)], 4: [(0, 4)], 7: [(1, 2)], 13: [(1, 3)], 14: [(2, 1)], 19: [(1, 4), (2, 2)]},
+    "project": {0: [(2, 0)], 1: [(3, 0)]},
+    "terms": {1: [(3, 1)], 3: [(2, 3)], 4: [(3, 2), (1, 5)]},
+    "far": {1: [(0, 5)]},
+    "near": {-1: [(3, 3), (2, 4)]},
+    "encoded": {-1: [(3, 4)], 0: [(2, 5)]},
+    "end": [(3, 5)],
 }
 
 
@@ -1727,12 +1726,12 @@
     acc_in, normal_in, inverse_in, turned_in, active_in, slope_in, far_ctx_in, *rest,
 ):
     encoded_out, input_out, small_out, *rest = rest
-    targets, rest = rest[:6], rest[6:]
+    targets, rest = rest[:4], rest[4:]
     enc_pair, grad_ref, input_far, acc, arrived, merge_recv, small, score_bias, *rest = rest
     chunk_grads, *rest = rest
-    grads, rest = [*[chunk_grads.at[p] for p in range(4)], *rest[:2]], rest[2:]
-    shards, rest = rest[:6], rest[6:]
-    buffers, rest = rest[: 6 * Scatter.buffers], rest[6 * Scatter.buffers :]
+    grads, rest = [*[chunk_grads.at[p] for p in range(2)], *rest[:2]], rest[2:]
+    shards, rest = rest[:4], rest[4:]
+    buffers, rest = rest[: 4 * Scatter.buffers], rest[4 * Scatter.buffers :]
     small_send, small_recv, in_sem, load_sem, ctx_sem, far_send, far_recv, merge_sem, enc_sem, input_sem, *sems = rest
     lines = Scatter(depth, grads, shards, targets, buffers, sems)
     sums = SmallSum(lines, small, small_send, small_recv)
@@ -1743,7 +1742,6 @@
     chunks, _, both = active_in.shape
     half = both // 2
     per_piece = chunks // 2
-    piece_span = grads[0].shape[1]
     pairs = qkv_in.shape[0]
     inner = pairs * PAIR
     tall, short = 256, 128
@@ -1847,10 +1845,10 @@
             )
 
         def own_columns(k):
-            return pl.ds(pl.multiple_of(lax.rem(k, per_piece) * half, half), half)
+            return pl.ds(pl.multiple_of(lax.rem(k, chunks) * half, half), half)
 
         def finish(k):
-            piece, slot = k // per_piece, lax.rem(k, 2)
+            piece, slot = k // chunks, lax.rem(k, 2)
             send(k).wait_recv()
 
             @pl.loop(0, width // tall)
@@ -1859,7 +1857,7 @@
                 chunk_grads[piece, at, own_columns(k)] += arrived[slot, at, :]
 
         def products(k, left, right):
-            piece, slot = k // per_piece, lax.rem(k, 2)
+            piece, slot = k // chunks, lax.rem(k, 2)
 
             @pl.when(k >= 2)
             def _():
@@ -1897,7 +1895,8 @@
                 acc[at, :] += dot_nt(grad, expand_buf[slot])
             for which, side in ((1 - member, 0), (member, half)):
                 row = 8 + which * 2 + j // per_piece
-                small[0, pl.ds(row, 1), own_columns(j)] = total[:, side : side + half]
+                spot = pl.ds(pl.multiple_of(lax.rem(j, per_piece) * half, half), half)
+                small[0, pl.ds(row, 1), spot] = total[:, side : side + half]
             products(chunks + j, turned, inner_grad)
 
         phase("reduce", chunks, reduce_chunk)
@@ -1946,7 +1945,7 @@
                 out_merge.wait()
                 for step in range(width // tall):
                     at = slice(step * tall, (step + 1) * tall)
-                    grads[4][at, 0:inner] = (
+                    grads[2][at, 0:inner] = (
                         dot_nn(turned[at, :], near_ctx[...]) + merge_recv[at, :].astype(WIDE)
                     ).astype(LOW)
 
@@ -2027,7 +2026,7 @@
                 )
 
             def project(second):
-                grad, first = (grads[5], 0) if second else (grads[4], inner)
+                grad, first = (grads[3], 0) if second else (grads[2], inner)
                 span = (pairs // 2) * 3 * PAIR
                 columns = slice(span if second else 0, span * 2 if second else span)
                 hidden_tile(0, 0).start()
@@ -2202,15 +2201,15 @@
 
 
 def finish_kernel(*refs):
-    sources, refs = refs[:27], refs[27:]
+    sources, refs = refs[:25], refs[25:]
     targets, refs = refs[:21], refs[21:]
-    held, made, (in_sem, out_sem) = refs[:27], refs[27:46], refs[46:]
-    loads = [pltpu.make_async_copy(sources[i], held[i], in_sem.at[i]) for i in range(27)]
+    held, made, (in_sem, out_sem) = refs[:25], refs[25:44], refs[44:]
+    loads = [pltpu.make_async_copy(sources[i], held[i], in_sem.at[i]) for i in range(25)]
     for copy in loads:
         copy.start()
     small_ref, *smalls = held[:7]
     vectors_ref, vectors_first, vectors_second, hidden_ref, hidden_first, hidden_second = smalls
-    shards, ins, rows_held = held[7:13], held[13:25], held[25:]
+    shards, ins, rows_held = held[7:11], held[11:23], held[23:]
     vector_grad_ref, *rest = made
     outs, small_out = rest[:12], rest[12:]
     results = [*rows_held, *made]
@@ -2245,20 +2244,18 @@
 
     for i in (2, *range(15, 21)):
         writes[i].start()
-    for copy in loads[7:13]:
+    for copy in loads[7:11]:
         copy.wait()
     for matrix in (3, 2, 1, 0):
-        for copy in loads[13 + 3 * matrix : 16 + 3 * matrix]:
+        for copy in loads[11 + 3 * matrix : 14 + 3 * matrix]:
             copy.wait()
         if matrix >= 2:
-            for i in range(2):
-                columns = slice(i * span, (i + 1) * span)
-                update(matrix, (), columns, shards[2 * (3 - matrix) + i], slice(0, span))
+            update(matrix, (), slice(0, span), shards[3 - matrix], slice(0, span))
         elif matrix == 1:
-            update(matrix, (), slice(0, inner), shards[4], slice(0, inner))
+            update(matrix, (), slice(0, inner), shards[2], slice(0, inner))
         else:
             for pair in range(pairs):
-                piece, begin = (4, inner) if pair < pairs // 2 else (5, 0)
+                piece, begin = (2, inner) if pair < pairs // 2 else (3, 0)
                 for c in range(3):
                     at = begin + (3 * (pair % (pairs // 2)) + c) * PAIR
                     columns = slice(pair * PAIR, (pair + 1) * PAIR)
@@ -2266,7 +2263,7 @@
         for copy in writes[3 + 3 * matrix : 6 + 3 * matrix]:
             copy.start()
         if matrix == 3:
-            for copy in loads[25:]:
+            for copy in loads[23:]:
                 copy.wait()
             for copy in writes[:2]:
                 copy.start()
@@ -2305,8 +2302,8 @@
     total_rows, inner = context.shape
     depth, shard_rows = parts // 4, width // parts
     half, pair_span = 256, 3 * PAIR * (qkv.shape[0] // 2)
-    piece_span = whole.shape[2] // 2
-    spans = (*[piece_span] * 4, inner + pair_span, pair_span)
+    piece_span = whole.shape[2]
+    spans = (*[piece_span] * 2, inner + pair_span, pair_span)
     classes = []
     for span in spans:
         third = max(128, span // 5 // 128 * 128)
@@ -2339,8 +2336,8 @@
             pltpu.VMEM((width, inner), LOW),
             pltpu.VMEM((2 * steps + 1, 16, width), WIDE),
             pltpu.VMEM((total_rows - LONGEST, total_rows - LONGEST), WIDE),
-            pltpu.VMEM((4, width, piece_span), LOW),
-            *[pltpu.VMEM((width, span), LOW) for span in spans[4:]],
+            pltpu.VMEM((2, width, piece_span), LOW),
+            *[pltpu.VMEM((width, span), LOW) for span in spans[2:]],
             *[pltpu.VMEM((shard_rows, span), WIDE) for span in spans],
             *Scatter.scratch(depth, shard_rows, classes),
             sem((steps,)),

time: 295 us -> 294 us (level)
  no operation moved by 1% of the time
where the time goes in v1:
time: 294 us; the launch traced here: 290 us
  Pallas kernels  289 us (98%)
    pallas_call x1, Pallas kernels, back(): pl.pallas_call(functools.partial(back_kernel, depth), in_specs=[*[pl.Bloc...  151 us
    pallas_call x1, Pallas kernels, front(): pl.pallas_call(functools.partial(front_kernel, depth), in_specs=[*[pl.Blo...  131 us
    pallas_call x1, Pallas kernels, finish(): pl.pallas_call(finish_kernel, in_specs=[anywhere] * len(operands), out_sp...  7.39 us

profile of v1, /device:TPU:0, one launch (start us, length us, event | category | flops | bytes accessed | tf_op | source)
XLA Modules:
  0.0 290.0 jit_solution(16851508431314383867)
XLA Ops:
  0.7 130.6 %shard_map.373 = (bf16[3,1024,2048]{2,1,0:T(8,128)(2,1)}, bf16[3,1024,2048]{2,1,0:T(8,128)(2,1)}, bf16[4,1536,384]{2,1,0:T(8,128)(2,1)}, bf16[1024,1536]{1,0:T(8...) custom-call(s32[1,4]{1,0:T(1,128)} %lengths_ref.3, ...), custom_call_target="tpu_custom_call" | custom-call | tf_op jit(solution)/shard_map/pallas_call | solution.py:891
  131.3 151.0 %shard_map.374 = (bf16[768,1024]{1,0:T(8,128)(2,1)}, bf16[768,1024]{1,0:T(8,128)(2,1)}, f32[16,1024]{1,0:T(8,128)}, f32[64,2048]{1,0:T(8,128)}, f32[64,2048]{1,0...) custom-call(s32[1,4]{1,0:T(1,128)} %lengths_ref.3, ...), custom_call_target="tpu_custom_call" | custom-call | tf_op jit(solution)/shard_map/pallas_call | solution.py:2316
  282.3 7.4 %shard_map.375 = (bf16[768,1024]{1,0:T(8,128)(2,1)}, bf16[768,1024]{1,0:T(8,128)(2,1)}, f32[8,1024]{1,0:T(8,128)}, f32[3,64,512]{2,1,0:T(8,128)}, f32[3,64,512]{...) custom-call(f32[16,1024]{1,0:T(8,128)} %get-tuple-element.77.refs_0_, ...), custom_call_target="tpu_custom_call" | custom-call | tf_op jit(solution)/shard_map/pallas_call | solution.py:2284
